TPU v7x, 512 devices: a whole 4x8x8 slice. The times are simulated.
512 devices in a mesh: row: 16 (over y, core), col: 32 (over x, z).
Axes of the slice: x: 4, y: 8, z: 8, core: 2. Of those that a mesh axis runs over, the one named last changes fastest.
Arguments:
- band_values: bfloat16 [2048, 64, 1536], P(('row', 'col')), may hold values from -0.3125 to 0.3125
- pattern: int32 [2048, 24], P(('row', 'col')), may hold values 0 or 1
Outputs:
- stepped: bfloat16 [2048, 64, 1536], P(('row', 'col'))
All inputs are finite; a program needn't handle non-finite values. No bound on the sum of `pattern` on one device may be relied on, other than what follows from the above.
Results may differ from a plain program's by a relative error of at most 0.0033.
Values may be sent and summed in bfloat16 or wider, within the bound.
No kernel may reach another device: no remote copies, remote signals or barrier semaphores. Data moves between devices by JAX's collectives and lax.ppermute only.
A program may use at most 192 MiB of HBM per device.

v0:
```python
import jax
import jax.numpy as jnp
from jax import lax
from jax.sharding import PartitionSpec as P


def from_behind(value, axis, steps):
    count = lax.axis_size(axis)
    pairs = [(source, (source + steps) % count) for source in range(count)]
    return lax.ppermute(value, axis, pairs)


def extend(own_panel, hop_count):
    beneath_parts = []
    above_parts = []
    lowered = own_panel
    raised = own_panel
    for offset in range(hop_count):
        lowered = from_behind(lowered, ("row", "col"), 1)
        raised = from_behind(raised, ("row", "col"), -1)
        beneath_parts.insert(0, lowered)
        above_parts.append(raised)
    return jnp.concatenate(beneath_parts + [own_panel] + above_parts, axis=0)


def band_product(left, extended, half_band):
    row_count, block_width, width_all = left.shape
    diagonals = width_all // block_width
    margin = half_band * block_width
    padded = jnp.pad(extended, ((0, 0), (0, 0), (margin, margin)))
    pieces = [
        padded[
            diag_index : diag_index + row_count,
            :,
            (diagonals - diag_index) * block_width : (2 * diagonals - diag_index) * block_width,
        ]
        for diag_index in range(diagonals)
    ]
    stacked = jnp.stack(pieces, axis=1).reshape(row_count, diagonals * block_width, width_all)
    return jnp.einsum("rak,rks->ras", left, stacked, preferred_element_type=jnp.float32)


def per_device(band_values, pattern):
    row_count, block_width, width_all = band_values.shape
    diagonals = width_all // block_width
    half_band = diagonals // 2
    hop_count = half_band // row_count
    keep = (pattern == 1)[:, None, :, None]
    shaped = band_values.reshape(row_count, block_width, diagonals, block_width)
    masked4 = jnp.where(keep, shaped, jnp.zeros_like(shaped))
    masked = masked4.reshape(row_count, block_width, width_all)
    square = band_product(masked, extend(masked, hop_count), half_band)
    square = square.reshape(row_count, block_width, diagonals, block_width)
    square = (
        jnp.where(keep, square, 0.0).astype(jnp.bfloat16).reshape(row_count, block_width, width_all)
    )
    cubic = band_product(masked, extend(square, hop_count), half_band)
    cubic = cubic.reshape(row_count, block_width, diagonals, block_width)
    result = jnp.where(keep, 1.5 * masked4.astype(jnp.float32) - 0.5 * cubic, 0.0)
    return result.astype(jnp.bfloat16).reshape(row_count, block_width, width_all)


def solution(mesh):
    placed = (P(("row", "col"), None, None), P(("row", "col"), None))
    return jax.shard_map(
        per_device,
        mesh=mesh,
        in_specs=placed,
        out_specs=P(("row", "col"), None, None),
        check_vma=False,
    )
```

profile of v0, /device:TPU:1, one launch (start us, length us, event | category | flops | bytes accessed | tf_op | source)
XLA Modules:
  0.0 202.5 jit_solution(4604478671979887435)
XLA Ops:
  2.1 4.8 %collective-permute-start = (bf16[4,64,1536]{2,1,0:T(8,128)(2,1)S(1)}, bf16[4,64,1536]{2,1,0:T(8,128)(2,1)S(1)}, u32[]{:S(2)}, u32[]{:S(2)}) collective-permute-start(bf16[4,64,1536]{2,1,0:T(8,128)(2,1)S(1)} %broadcast_select_fusion), channel_id=1, source_target_pairs={{0,1},{1,2},{2,3},{3,4},{4,5},{5,6},{6,7},{7,8},{8,9},{9,10},{10,1... | collective-permute-start | bytes 2359304 | tf_op jit(solution)/shard_map/ppermute | solution.py:10
  6.9 11.3 %collective-permute-start.3 = (bf16[4,64,1536]{2,1,0:T(8,128)(2,1)S(1)}, bf16[4,64,1536]{2,1,0:T(8,128)(2,1)S(1)}, u32[]{:S(2)}, u32[]{:S(2)}) collective-permute-start(bf16[4,64,1536]{2,1,0:T(8,128)(2,1)S(1)} %broadcast_select_fusion), channel_id=1, source_target_pairs={{0,511},{1,0},{2,1},{3,2},{4,3},{5,4},{6,5},{7,6},{8,7},{9,8},{10,... | collective-permute-start | bytes 2359304 | tf_op jit(solution)/shard_map/ppermute | solution.py:10
  18.3 16.2 %collective-permute-done = bf16[4,64,1536]{2,1,0:T(8,128)(2,1)S(1)} collective-permute-done((bf16[4,64,1536]{2,1,0:T(8,128)(2,1)S(1)}, bf16[4,64,1536]{2,1,0:T(8,128)(2,1)S(1)}, u32[]{:S(2)}, u32[]{:S(2)}) %collective-permute-start) | collective-permute-done | bytes 786464 | tf_op jit(solution)/shard_map/ppermute | solution.py:10
  34.4 1.9 collective-permute-start.1
  36.3 7.0 %collective-permute-start.4 = (bf16[4,64,1536]{2,1,0:T(8,128)(2,1)S(1)}, bf16[4,64,1536]{2,1,0:T(8,128)(2,1)S(1)}, u32[]{:S(2)}, u32[]{:S(2)}) collective-permute-start(bf16[4,64,1536]{2,1,0:T(8,128)(2,1)S(1)} %collective-permute-done.3), channel_id=1, source_target_pairs={{0,511},{1,0},{2,1},{3,2},{4,3},{5,4},{6,5},{7,6},{8,7},{9,8},{10,... | collective-permute-start | bytes 2359304 | tf_op jit(solution)/shard_map/ppermute | solution.py:10
  43.3 13.4 %collective-permute-done.1 = bf16[4,64,1536]{2,1,0:T(8,128)(2,1)S(1)} collective-permute-done((bf16[4,64,1536]{2,1,0:T(8,128)(2,1)S(1)}, bf16[4,64,1536]{2,1,0:T(8,128)(2,1)S(1)}, u32[]{:S(2)}, u32[]{:S(2)}) %collective-permute-start.1) | collective-permute-done | bytes 786464 | tf_op jit(solution)/shard_map/ppermute | solution.py:10
  56.8 1.9 collective-permute-start.2
  58.7 7.0 %collective-permute-start.5 = (bf16[4,64,1536]{2,1,0:T(8,128)(2,1)S(1)}, bf16[4,64,1536]{2,1,0:T(8,128)(2,1)S(1)}, u32[]{:S(2)}, u32[]{:S(2)}) collective-permute-start(bf16[4,64,1536]{2,1,0:T(8,128)(2,1)S(1)} %collective-permute-done.4), channel_id=1, source_target_pairs={{0,511},{1,0},{2,1},{3,2},{4,3},{5,4},{6,5},{7,6},{8,7},{9,8},{10,... | collective-permute-start | bytes 2359304 | tf_op jit(solution)/shard_map/ppermute | solution.py:10
  65.7 10.5 %collective-permute-done.2 = bf16[4,64,1536]{2,1,0:T(8,128)(2,1)S(1)} collective-permute-done((bf16[4,64,1536]{2,1,0:T(8,128)(2,1)S(1)}, bf16[4,64,1536]{2,1,0:T(8,128)(2,1)S(1)}, u32[]{:S(2)}, u32[]{:S(2)}) %collective-permute-start.2) | collective-permute-done | bytes 786464 | tf_op jit(solution)/shard_map/ppermute | solution.py:10
  103.3 9.7 %copy.4 = bf16[4,24,64,1536]{3,2,1,0:T(8,128)(2,1)S(1)} copy(bf16[4,24,64,1536]{3,2,0,1:T(8,128)(2,1)} %fusion.49) | data formatting | bytes 37748736 | tf_op jit(solution)/shard_map/stack | solution.py:39
  113.0 3.3 %fusion.3 = bf16[4,64,1536]{2,1,0:T(8,128)(2,1)S(1)} fusion(bf16[4,1536,1536]{2,1,0:T(8,128)(2,1)S(1)} %bitcast.194, pred[4,1536]{1,0:T(4,128)(4,1)S(1)} %broadcast_in_dim.31, bf16[4,64,1536]{2,1,0:T(8,128)(2,1)S(1)} %copy-done), kind=kOutput, calls=%fused_computation.51 | convolution fusion | flops 1209139200 | bytes 20453376 | tf_op jit(solution)/shard_map/rak,rks->ras/dot_general | solution.py:40
  116.3 1.9 collective-permute-start.6
  118.2 7.0 %collective-permute-start.9 = (bf16[4,64,1536]{2,1,0:T(8,128)(2,1)S(1)}, bf16[4,64,1536]{2,1,0:T(8,128)(2,1)S(1)}, u32[]{:S(2)}, u32[]{:S(2)}) collective-permute-start(bf16[4,64,1536]{2,1,0:T(8,128)(2,1)S(1)} %fusion.3), channel_id=1, source_target_pairs={{0,511},{1,0},{2,1},{3,2},{4,3},{5,4},{6,5},{7,6},{8,7},{9,8},{10,... | collective-permute-start | bytes 2359304 | tf_op jit(solution)/shard_map/ppermute | solution.py:10
  125.2 10.3 %collective-permute-done.6 = bf16[4,64,1536]{2,1,0:T(8,128)(2,1)S(1)} collective-permute-done((bf16[4,64,1536]{2,1,0:T(8,128)(2,1)S(1)}, bf16[4,64,1536]{2,1,0:T(8,128)(2,1)S(1)}, u32[]{:S(2)}, u32[]{:S(2)}) %collective-permute-start.6) | collective-permute-done | bytes 786464 | tf_op jit(solution)/shard_map/ppermute | solution.py:10
  135.5 1.9 collective-permute-start.7
  137.5 6.8 %collective-permute-start.10 = (bf16[4,64,1536]{2,1,0:T(8,128)(2,1)S(1)}, bf16[4,64,1536]{2,1,0:T(8,128)(2,1)S(1)}, u32[]{:S(2)}, u32[]{:S(2)}) collective-permute-start(bf16[4,64,1536]{2,1,0:T(8,128)(2,1)S(1)} %collective-permute-done.9), channel_id=1, source_target_pairs={{0,511},{1,0},{2,1},{3,2},{4,3},{5,4},{6,5},{7,6},{8,7},{9,8},{10,... | collective-permute-start | bytes 2359304 | tf_op jit(solution)/shard_map/ppermute | solution.py:10
  144.4 11.9 %collective-permute-done.7 = bf16[4,64,1536]{2,1,0:T(8,128)(2,1)S(1)} collective-permute-done((bf16[4,64,1536]{2,1,0:T(8,128)(2,1)S(1)}, bf16[4,64,1536]{2,1,0:T(8,128)(2,1)S(1)}, u32[]{:S(2)}, u32[]{:S(2)}) %collective-permute-start.7) | collective-permute-done | bytes 786464 | tf_op jit(solution)/shard_map/ppermute | solution.py:10
  156.3 1.9 collective-permute-start.8
  158.2 1.4 collective-permute-done.10
  159.6 7.9 %collective-permute-start.11 = (bf16[4,64,1536]{2,1,0:T(8,128)(2,1)S(1)}, bf16[4,64,1536]{2,1,0:T(8,128)(2,1)S(1)}, u32[]{:S(2)}, u32[]{:S(2)}) collective-permute-start(bf16[4,64,1536]{2,1,0:T(8,128)(2,1)S(1)} %collective-permute-done.10), channel_id=1, source_target_pairs={{0,511},{1,0},{2,1},{3,2},{4,3},{5,4},{6,5},{7,6},{8,7},{9,8},{10,... | collective-permute-start | bytes 2359304 | tf_op jit(solution)/shard_map/ppermute | solution.py:10
  167.5 8.0 %collective-permute-done.8 = bf16[4,64,1536]{2,1,0:T(8,128)(2,1)S(1)} collective-permute-done((bf16[4,64,1536]{2,1,0:T(8,128)(2,1)S(1)}, bf16[4,64,1536]{2,1,0:T(8,128)(2,1)S(1)}, u32[]{:S(2)}, u32[]{:S(2)}) %collective-permute-start.8) | collective-permute-done | bytes 786464 | tf_op jit(solution)/shard_map/ppermute | solution.py:10
  175.8 5.4 %collective-permute-done.11 = bf16[4,64,1536]{2,1,0:T(8,128)(2,1)S(1)} collective-permute-done((bf16[4,64,1536]{2,1,0:T(8,128)(2,1)S(1)}, bf16[4,64,1536]{2,1,0:T(8,128)(2,1)S(1)}, u32[]{:S(2)}, u32[]{:S(2)}) %collective-permute-start.11) | collective-permute-done | bytes 786464 | tf_op jit(solution)/shard_map/ppermute | solution.py:10
  185.1 6.8 %copy.5 = bf16[4,24,64,1536]{3,2,1,0:T(8,128)(2,1)} copy(bf16[4,24,64,1536]{3,2,0,1:T(8,128)(2,1)S(1)} %fusion.95) | data formatting | bytes 37748736 | tf_op jit(solution)/shard_map/stack | solution.py:39
  191.9 10.6 %fusion.2 = bf16[4,64,1536]{2,1,0:T(8,128)(2,1)} fusion(bf16[4,1536,1536]{2,1,0:T(8,128)(2,1)} %bitcast.195, pred[4,1536]{1,0:T(4,128)(4,1)S(1)} %broadcast_in_dim.31, bf16[4,64,1536]{2,1,0:T(8,128)(2,1)S(1)} %copy-done), kind=kOutput, calls=%fused_computation.50 | convolution fusion | flops 1211105280 | bytes 20453376 | tf_op jit(solution)/shard_map/rak,rks->ras/dot_general | solution.py:40
  (72 shorter events, 33.4 us)
Async XLA Ops:
  2.1 32.3 %collective-permute-start = (bf16[4,64,1536]{2,1,0:T(8,128)(2,1)S(1)}, bf16[4,64,1536]{2,1,0:T(8,128)(2,1)S(1)}, u32[]{:S(2)}, u32[]{:S(2)}) collective-permute-start(bf16[4,64,1536]{2,1,0:T(8,128)(2,1)S(1)} %broadcast_select_fusion), channel_id=1, source_target_pairs={{0,1},{1,2},{2,3},{3,4},{4,5},{5,6},{6,7},{7,8},{8,9},{9,10},{10,1... | collective-permute-start | bytes 2359304 | tf_op jit(solution)/shard_map/ppermute | solution.py:10
  6.9 29.4 %collective-permute-start.3 = (bf16[4,64,1536]{2,1,0:T(8,128)(2,1)S(1)}, bf16[4,64,1536]{2,1,0:T(8,128)(2,1)S(1)}, u32[]{:S(2)}, u32[]{:S(2)}) collective-permute-start(bf16[4,64,1536]{2,1,0:T(8,128)(2,1)S(1)} %broadcast_select_fusion), channel_id=1, source_target_pairs={{0,511},{1,0},{2,1},{3,2},{4,3},{5,4},{6,5},{7,6},{8,7},{9,8},{10,... | collective-permute-start | bytes 2359304 | tf_op jit(solution)/shard_map/ppermute | solution.py:10
  34.4 22.3 %collective-permute-start.1 = (bf16[4,64,1536]{2,1,0:T(8,128)(2,1)S(1)}, bf16[4,64,1536]{2,1,0:T(8,128)(2,1)S(1)}, u32[]{:S(2)}, u32[]{:S(2)}) collective-permute-start(bf16[4,64,1536]{2,1,0:T(8,128)(2,1)S(1)} %collective-permute-done), channel_id=1, source_target_pairs={{0,1},{1,2},{2,3},{3,4},{4,5},{5,6},{6,7},{7,8},{8,9},{9,10},{10,1... | collective-permute-start | bytes 2359304 | tf_op jit(solution)/shard_map/ppermute | solution.py:10
  36.3 22.3 %collective-permute-start.4 = (bf16[4,64,1536]{2,1,0:T(8,128)(2,1)S(1)}, bf16[4,64,1536]{2,1,0:T(8,128)(2,1)S(1)}, u32[]{:S(2)}, u32[]{:S(2)}) collective-permute-start(bf16[4,64,1536]{2,1,0:T(8,128)(2,1)S(1)} %collective-permute-done.3), channel_id=1, source_target_pairs={{0,511},{1,0},{2,1},{3,2},{4,3},{5,4},{6,5},{7,6},{8,7},{9,8},{10,... | collective-permute-start | bytes 2359304 | tf_op jit(solution)/shard_map/ppermute | solution.py:10
  56.8 19.4 %collective-permute-start.2 = (bf16[4,64,1536]{2,1,0:T(8,128)(2,1)S(1)}, bf16[4,64,1536]{2,1,0:T(8,128)(2,1)S(1)}, u32[]{:S(2)}, u32[]{:S(2)}) collective-permute-start(bf16[4,64,1536]{2,1,0:T(8,128)(2,1)S(1)} %collective-permute-done.1), channel_id=1, source_target_pairs={{0,1},{1,2},{2,3},{3,4},{4,5},{5,6},{6,7},{7,8},{8,9},{9,10},{10,1... | collective-permute-start | bytes 2359304 | tf_op jit(solution)/shard_map/ppermute | solution.py:10
  58.7 19.0 %collective-permute-start.5 = (bf16[4,64,1536]{2,1,0:T(8,128)(2,1)S(1)}, bf16[4,64,1536]{2,1,0:T(8,128)(2,1)S(1)}, u32[]{:S(2)}, u32[]{:S(2)}) collective-permute-start(bf16[4,64,1536]{2,1,0:T(8,128)(2,1)S(1)} %collective-permute-done.4), channel_id=1, source_target_pairs={{0,511},{1,0},{2,1},{3,2},{4,3},{5,4},{6,5},{7,6},{8,7},{9,8},{10,... | collective-permute-start | bytes 2359304 | tf_op jit(solution)/shard_map/ppermute | solution.py:10
  84.0 6.6 %copy-start = (bf16[4,64,1536]{2,1,0:T(8,128)(2,1)S(1)}, bf16[4,64,1536]{2,1,0:T(8,128)(2,1)}, u32[]{:S(2)}) copy-start(bf16[4,64,1536]{2,1,0:T(8,128)(2,1)} %param.2) | copy-start | bytes 2359300
  116.3 19.2 %collective-permute-start.6 = (bf16[4,64,1536]{2,1,0:T(8,128)(2,1)S(1)}, bf16[4,64,1536]{2,1,0:T(8,128)(2,1)S(1)}, u32[]{:S(2)}, u32[]{:S(2)}) collective-permute-start(bf16[4,64,1536]{2,1,0:T(8,128)(2,1)S(1)} %fusion.3), channel_id=1, source_target_pairs={{0,1},{1,2},{2,3},{3,4},{4,5},{5,6},{6,7},{7,8},{8,9},{9,10},{10,1... | collective-permute-start | bytes 2359304 | tf_op jit(solution)/shard_map/ppermute | solution.py:10
  118.2 19.3 %collective-permute-start.9 = (bf16[4,64,1536]{2,1,0:T(8,128)(2,1)S(1)}, bf16[4,64,1536]{2,1,0:T(8,128)(2,1)S(1)}, u32[]{:S(2)}, u32[]{:S(2)}) collective-permute-start(bf16[4,64,1536]{2,1,0:T(8,128)(2,1)S(1)} %fusion.3), channel_id=1, source_target_pairs={{0,511},{1,0},{2,1},{3,2},{4,3},{5,4},{6,5},{7,6},{8,7},{9,8},{10,... | collective-permute-start | bytes 2359304 | tf_op jit(solution)/shard_map/ppermute | solution.py:10
  135.5 20.8 %collective-permute-start.7 = (bf16[4,64,1536]{2,1,0:T(8,128)(2,1)S(1)}, bf16[4,64,1536]{2,1,0:T(8,128)(2,1)S(1)}, u32[]{:S(2)}, u32[]{:S(2)}) collective-permute-start(bf16[4,64,1536]{2,1,0:T(8,128)(2,1)S(1)} %collective-permute-done.6), channel_id=1, source_target_pairs={{0,1},{1,2},{2,3},{3,4},{4,5},{5,6},{6,7},{7,8},{8,9},{9,10},{10,1... | collective-permute-start | bytes 2359304 | tf_op jit(solution)/shard_map/ppermute | solution.py:10
  137.5 22.1 %collective-permute-start.10 = (bf16[4,64,1536]{2,1,0:T(8,128)(2,1)S(1)}, bf16[4,64,1536]{2,1,0:T(8,128)(2,1)S(1)}, u32[]{:S(2)}, u32[]{:S(2)}) collective-permute-start(bf16[4,64,1536]{2,1,0:T(8,128)(2,1)S(1)} %collective-permute-done.9), channel_id=1, source_target_pairs={{0,511},{1,0},{2,1},{3,2},{4,3},{5,4},{6,5},{7,6},{8,7},{9,8},{10,... | collective-permute-start | bytes 2359304 | tf_op jit(solution)/shard_map/ppermute | solution.py:10
  156.3 19.2 %collective-permute-start.8 = (bf16[4,64,1536]{2,1,0:T(8,128)(2,1)S(1)}, bf16[4,64,1536]{2,1,0:T(8,128)(2,1)S(1)}, u32[]{:S(2)}, u32[]{:S(2)}) collective-permute-start(bf16[4,64,1536]{2,1,0:T(8,128)(2,1)S(1)} %collective-permute-done.7), channel_id=1, source_target_pairs={{0,1},{1,2},{2,3},{3,4},{4,5},{5,6},{6,7},{7,8},{8,9},{9,10},{10,1... | collective-permute-start | bytes 2359304 | tf_op jit(solution)/shard_map/ppermute | solution.py:10
  159.6 21.6 %collective-permute-start.11 = (bf16[4,64,1536]{2,1,0:T(8,128)(2,1)S(1)}, bf16[4,64,1536]{2,1,0:T(8,128)(2,1)S(1)}, u32[]{:S(2)}, u32[]{:S(2)}) collective-permute-start(bf16[4,64,1536]{2,1,0:T(8,128)(2,1)S(1)} %collective-permute-done.10), channel_id=1, source_target_pairs={{0,511},{1,0},{2,1},{3,2},{4,3},{5,4},{6,5},{7,6},{8,7},{9,8},{10,... | collective-permute-start | bytes 2359304 | tf_op jit(solution)/shard_map/ppermute | solution.py:10
where the time goes:
time: 205 us; the launch traced here: 202 us
  waiting for transfers between devices  77.2 us (38%)
  starting transfers between devices  61.3 us (30%)
  local copies, waits for them, and re-layouts  45.4 us (22%)
  matrix products  13.9 us (7%)
  other arithmetic  4.2 us (2%)
    ppermute x12, waiting for transfers between devices, from_behind(): return lax.ppermute(value, axis, pairs)  77.2 us
    ppermute x12, starting transfers between devices, from_behind(): return lax.ppermute(value, axis, pairs)  61.3 us
    unnamed x58, local copies, waits for them, and re-layouts  27.5 us
    another operation x4, local copies, waits for them, and re-layouts, band_product(): jnp.stack(pieces, axis=1)  17.7 us
    dot_general x2, matrix products, band_product(): jnp.einsum('rak,rks->ras', left, stacked, preferred_element_type=jnp.floa...  13.9 us
  transfers between devices with their start and end apart: 12, of which 9 were waited for; matrix products, arithmetic and copies ran while one was open for 1% of the time, Pallas kernels for 0%

commit v1 on v0

v1 whole, which is shorter than its diff:
```python
import functools

import jax
import jax.numpy as jnp
from jax import lax
from jax.experimental import pallas as pl
from jax.experimental.pallas import tpu as pltpu
from jax.sharding import PartitionSpec as P

AXES = ("row", "col")
BLOCK = 64
ROWS = 4
TILE = ROWS * BLOCK
REACH = 3
TILES = 2 * REACH + 1
HEAD = 5 * BLOCK
BODY = 10 * TILE
TAIL = 3 * BLOCK
DATA = HEAD + BODY + TAIL
NOTE = 16
ALL = DATA + NOTE
F32 = jnp.float32
BF16 = jnp.bfloat16
VMEM = pl.BlockSpec(memory_space=pltpu.VMEM)
SMEM = pl.BlockSpec(memory_space=pltpu.SMEM)


def first_rows(tiles):
    return HEAD + (tiles - 1) * 2 * TILE


def last_rows(tiles):
    return TAIL + (tiles - 1) * 2 * TILE


def half_lanes(rows):
    return lax.broadcasted_iota(jnp.int32, (rows, 128), 1) < BLOCK


def swap_halves(piece):
    return pltpu.roll(piece.astype(F32), BLOCK, 1)


def pack_kernel(x_ref, pattern_ref, out_ref):
    low = half_lanes(BLOCK)
    zero = jnp.zeros((BLOCK, 128), F32)
    note = jnp.zeros((NOTE, 128), F32)
    lane = lax.broadcasted_iota(jnp.int32, (NOTE, 128), 1)
    row = lax.broadcasted_iota(jnp.int32, (NOTE, 128), 0)
    slots = x_ref.shape[2] // BLOCK
    strips = []
    for q in range(ROWS):
        pieces = []
        for pair in range(slots // 2):
            even = pattern_ref[q, 2 * pair]
            odd = pattern_ref[q, 2 * pair + 1]
            keep = jnp.where(low, even, odd) == 1
            piece = x_ref[q, :, pair * 128 : (pair + 1) * 128].astype(F32)
            pieces.append(jnp.where(keep, piece, 0.0))
            for slot, present in ((2 * pair, even), (2 * pair + 1, odd)):
                value = jnp.where(present == 1, 1.0, 0.0)
                note = jnp.where((row == q) & (lane == slot + q), value, note)
        shifted = [zero] * (q // 2)
        if q % 2 == 0:
            shifted += pieces
        else:
            turned = [swap_halves(piece) for piece in pieces]
            shifted.append(jnp.where(low, 0.0, turned[0]))
            for left, right in zip(turned[:-1], turned[1:]):
                shifted.append(jnp.where(low, left, right))
            shifted.append(jnp.where(low, turned[-1], 0.0))
        shifted += [zero] * (2 * TILES - len(shifted))
        strips.append(shifted)

    def put(start, piece):
        out_ref[start : start + BLOCK, :] = piece.astype(BF16)

    put(0, strips[0][0])
    put(BLOCK, strips[0][1])
    put(2 * BLOCK, strips[1][1])
    put(3 * BLOCK, strips[2][1])
    put(4 * BLOCK, jnp.where(low, swap_halves(strips[3][1]), strips[1][0]))
    for pair in range(2, 2 * TILES - 2):
        for q in range(ROWS):
            put(HEAD + (pair - 2) * TILE + q * BLOCK, strips[q][pair])
    put(HEAD + BODY, strips[2][2 * TILES - 2])
    put(HEAD + BODY + BLOCK, strips[3][2 * TILES - 2])
    put(
        HEAD + BODY + 2 * BLOCK,
        jnp.where(low, strips[1][2 * TILES - 2], swap_halves(strips[3][2 * TILES - 1])),
    )
    out_ref[DATA:, :] = note.astype(BF16)


def pack(x, pattern):
    return pl.pallas_call(
        pack_kernel,
        out_shape=jax.ShapeDtypeStruct((ALL, 128), BF16),
        in_specs=[VMEM, SMEM],
        out_specs=VMEM,
        compiler_params=pltpu.CompilerParams(vmem_limit_bytes=32 << 20),
        cost_estimate=pl.CostEstimate(flops=1 << 20, bytes_accessed=3 << 20, transcendentals=0),
    )(x, pattern)


def unpack_tile(source, tile, base, window, row, col):
    def put(q, half, piece):
        window[pl.ds(row + q * BLOCK, BLOCK), pl.ds(col + half * 128, 128)] = piece

    low = half_lanes(BLOCK)
    zero = jnp.zeros((BLOCK, 128), BF16)
    if tile == 0:

        def seg(k):
            return source[base + k * BLOCK : base + (k + 1) * BLOCK, :]

        mixed = seg(4)
        put(0, 0, seg(0))
        put(0, 1, seg(1))
        put(1, 0, jnp.where(low, 0.0, mixed.astype(F32)).astype(BF16))
        put(1, 1, seg(2))
        put(2, 0, zero)
        put(2, 1, seg(3))
        put(3, 0, zero)
        put(3, 1, jnp.where(low, 0.0, swap_halves(mixed)).astype(BF16))
    elif tile == TILES - 1:

        def seg(k):
            return source[base + k * BLOCK : base + (k + 1) * BLOCK, :]

        mixed = seg(2)
        put(0, 0, zero)
        put(0, 1, zero)
        put(1, 0, jnp.where(low, mixed.astype(F32), 0.0).astype(BF16))
        put(1, 1, zero)
        put(2, 0, seg(0))
        put(2, 1, zero)
        put(3, 0, seg(1))
        put(3, 1, jnp.where(low, swap_halves(mixed), 0.0).astype(BF16))
    else:
        for half in range(2):
            start = base + half * TILE
            window[row : row + TILE, col + half * 128 : col + half * 128 + 128] = source[start : start + TILE, :]


def tile_start(tile, first):
    def whole(t):
        return 0 if t == 0 else HEAD + (t - 1) * 2 * TILE

    return whole(tile) - whole(first)


def spread(note):
    lane = lax.broadcasted_iota(jnp.int32, (128, TILES * TILE), 1) // BLOCK
    block = lax.broadcasted_iota(jnp.int32, (128, TILES * TILE), 0)
    return jnp.dot(note, jnp.where(lane == block, 1.0, 0.0).astype(BF16), preferred_element_type=F32)


def square_tiles(pairs, lowest, window, notes, square):
    for k, c in pairs:
        first, last = max(k, c) - REACH, min(k, c) + REACH
        depth = slice((first - lowest) * TILE, (last + 1 - lowest) * TILE)
        total = jnp.dot(
            window[(k - lowest) * TILE : (k + 1 - lowest) * TILE, depth],
            window[depth, (c - lowest) * TILE : (c + 1 - lowest) * TILE],
            preferred_element_type=F32,
        )
        place = (c - k + REACH) * TILE
        for q in range(ROWS):
            keep = notes[k][q : q + 1, place : place + TILE] > 0.5
            square[
                pl.ds((k + REACH) * TILE + q * BLOCK, BLOCK), pl.ds((c + REACH) * TILE, TILE)
            ] = jnp.where(keep, total[q * BLOCK : (q + 1) * BLOCK], 0.0).astype(BF16)


MIDDLE = [(k, c) for k in range(-REACH, REACH + 1) for c in range(-REACH, REACH + 1) if k * c <= 0 and abs(k - c) <= REACH]
LOWER = [(k, c) for k in range(-REACH, 0) for c in range(-REACH, 0)]
UPPER = [(-k, -c) for k, c in LOWER]


def needed(pairs):
    found = set()
    for k, c in pairs:
        for l in range(max(k, c) - REACH, min(k, c) + REACH + 1):
            found.add((k, l))
            found.add((l, c))
    return sorted(found)


def middle_kernel(*refs):
    messages = dict(zip(range(-REACH, REACH + 1), refs[:TILES]))
    out_ref, window, square = refs[TILES:]
    for r, t in needed(MIDDLE):
        j = t - r + REACH
        unpack_tile(
            messages[r], j, tile_start(j, 0), window, (r + REACH) * TILE, (t + REACH) * TILE
        )
    notes = {k: spread(messages[k][DATA:, :]) for k in messages}
    square_tiles(MIDDLE, -REACH, window, notes, square)
    own = slice(REACH * TILE, (REACH + 1) * TILE)
    for c in range(-REACH, REACH + 1):
        rows = [k for k, other in MIDDLE if other == c]
        depth = slice((min(rows) + REACH) * TILE, (max(rows) + REACH + 1) * TILE)
        cols = slice((c + REACH) * TILE, (c + REACH + 1) * TILE)
        out_ref[:, cols] = jnp.dot(window[own, depth], square[depth, cols], preferred_element_type=F32)


def middle(messages):
    flops = 112 * 2 * TILE**3
    return pl.pallas_call(
        middle_kernel,
        out_shape=jax.ShapeDtypeStruct((TILE, TILES * TILE), F32),
        in_specs=[VMEM] * TILES,
        out_specs=VMEM,
        scratch_shapes=[
            pltpu.VMEM((TILES * TILE, TILES * TILE), BF16),
            pltpu.VMEM((TILES * TILE, TILES * TILE), BF16),
        ],
        compiler_params=pltpu.CompilerParams(vmem_limit_bytes=48 << 20),
        cost_estimate=pl.CostEstimate(flops=flops, bytes_accessed=8 << 20, transcendentals=0),
    )(*messages)


FAR = 2 * REACH
SPAN = 2 * FAR + 1


def corner_kernel(*refs):
    messages = dict(zip(range(-FAR, FAR + 1), refs[:SPAN]))
    part_ref, pattern_ref, out_ref, window, square = refs[SPAN:]
    for r, t in sorted(set(needed(LOWER + UPPER)) | {(0, t) for t in range(-REACH, REACH + 1)}):
        j = t - r + REACH
        first = -r if -r > REACH else 0
        unpack_tile(messages[r], j, tile_start(j, first), window, (r + FAR) * TILE, (t + FAR) * TILE)
    notes = {k: spread(messages[k][DATA:, :]) for k in range(-REACH, REACH + 1)}
    square_tiles(LOWER + UPPER, -FAR, window, notes, square)
    own = slice(FAR * TILE, (FAR + 1) * TILE)
    keep_own = notes[0]
    steps = []
    for c in range(-REACH, REACH + 1):
        cols = slice((c + REACH) * TILE, (c + REACH + 1) * TILE)
        part = part_ref[:, cols]
        if c:
            rows = (-REACH, -1) if c < 0 else (1, REACH)
            part = part + jnp.dot(
                window[own, (rows[0] + FAR) * TILE : (rows[1] + FAR + 1) * TILE],
                square[(rows[0] + REACH) * TILE : (rows[1] + REACH + 1) * TILE, cols],
                preferred_element_type=F32,
            )
        x = window[own, (c + FAR) * TILE : (c + FAR + 1) * TILE].astype(F32)
        steps.append(1.5 * x - 0.5 * part)
    width = out_ref.shape[2]
    for q in range(ROWS):
        rows = slice(q * BLOCK, (q + 1) * BLOCK)
        strip = jnp.concatenate([step[rows] for step in steps], axis=1)
        strip = jnp.where(keep_own[q : q + 1] > 0.5, strip, 0.0)
        if q % 2:
            strip = pltpu.roll(strip, TILES * TILE - BLOCK, 1)
        start = (q // 2) * 128
        out_ref[q] = strip[:, start : start + width].astype(BF16)


def corners(messages, part, pattern, out_type):
    flops = 128 * 2 * TILE**3
    return pl.pallas_call(
        corner_kernel,
        out_shape=out_type,
        in_specs=[VMEM] * (SPAN + 1) + [SMEM],
        out_specs=VMEM,
        scratch_shapes=[
            pltpu.VMEM((SPAN * TILE, SPAN * TILE), BF16),
            pltpu.VMEM((TILES * TILE, TILES * TILE), BF16),
        ],
        compiler_params=pltpu.CompilerParams(vmem_limit_bytes=56 << 20),
        cost_estimate=pl.CostEstimate(flops=flops, bytes_accessed=12 << 20, transcendentals=0),
    )(*messages, part, pattern)


def per_device(count, x, pattern):
    up = [(n, (n + 1) % count) for n in range(count)]
    down = [(n, (n - 1) % count) for n in range(count)]
    own = pack(x, pattern)
    below = own
    above = own
    held = {0: own}
    for step in range(1, REACH + 1):
        below = lax.ppermute(below, AXES, up)
        above = lax.ppermute(above, AXES, down)
        held[-step], held[step] = below, above
    part = middle([held[k] for k in range(-REACH, REACH + 1)])
    below = below[DATA - last_rows(REACH) : DATA]
    above = above[: first_rows(REACH)]
    for step in range(REACH + 1, FAR + 1):
        tiles = FAR + 1 - step
        below = lax.ppermute(below[below.shape[0] - last_rows(tiles) :], AXES, up)
        above = lax.ppermute(above[: first_rows(tiles)], AXES, down)
        if step == REACH + 1:
            below, part = lax.optimization_barrier((below, part))
        held[-step], held[step] = below, above
    return corners(
        [held[k] for k in range(-FAR, FAR + 1)], part, pattern, jax.ShapeDtypeStruct(x.shape, x.dtype)
    )


def solution(mesh):
    placed = (P(AXES, None, None), P(AXES, None))
    count = mesh.shape["row"] * mesh.shape["col"]
    return jax.shard_map(
        functools.partial(per_device, count),
        mesh=mesh,
        in_specs=placed,
        out_specs=P(AXES, None, None),
        check_vma=False,
    )
```

time: 205 us -> 130 us (0.63); the launches traced: 202 us -> 130 us
  local copies, waits for them, and re-layouts: 45.4 us -> 3.16 us
  waiting for transfers between devices: 77.2 us -> 47.4 us
  Pallas kernels: 0 us -> 16 us
  matrix products: 13.9 us -> 0 us
  other arithmetic: 4.2 us -> 0 us
    ppermute x12, waiting for transfers between devices: 77.2 us -> 47.4 us  [the longest x3 29.5 us: per_device(): above = lax.ppermute(above, AXES, down)]
    unnamed x58 -> x30, local copies, waits for them, and re-layouts: 27.5 us -> 3.07 us
    another operation x4 -> x0, local copies, waits for them, and re-layouts: 17.7 us -> none  [band_product(): jnp.stack(pieces, axis=1)]
    pallas_call x0 -> x3, Pallas kernels: none -> 16 us  [the longest x1 9.59 us: corners(): pl.pallas_call(corner_kernel, out_shape=out_type, in_specs=[VMEM] * (SPAN...]
    dot_general x2 -> x0, matrix products: 13.9 us -> none  [band_product(): jnp.einsum('rak,rks->ras', left, stacked, preferred_element_type=jnp.floa...]
    unnamed x2 -> x0, other arithmetic: 2.31 us -> none
  transfers between devices with their start and end apart: 12 -> 12, of which waited for: 9 -> 7; matrix products, arithmetic and copies ran while one was open for 1% -> 0% of each run, Pallas kernels for 0% -> 4%
where the time goes in v1:
time: 130 us
  starting transfers between devices  62.8 us (48%)
  waiting for transfers between devices  47.4 us (36%)
  Pallas kernels  16 us (12%)
  local copies, waits for them, and re-layouts  3.16 us (2%)
    ppermute x3, starting transfers between devices, per_device(): above = lax.ppermute(above, AXES, down)  29.6 us
    ppermute x3, waiting for transfers between devices, per_device(): above = lax.ppermute(above, AXES, down)  29.5 us
    ppermute x3, starting transfers between devices, per_device(): above = lax.ppermute(above[:first_rows(tiles)], AXES, down)  21.6 us
    pallas_call x1, Pallas kernels, corners(): pl.pallas_call(corner_kernel, out_shape=out_type, in_specs=[VMEM] * (SPAN...  9.59 us
    ppermute x3, waiting for transfers between devices, per_device(): below = lax.ppermute(below[below.shape[0] - last_rows(tiles):], AXES, up)  9.28 us
    ppermute x3, waiting for transfers between devices, per_device(): below = lax.ppermute(below, AXES, up)  8.58 us
    ppermute x3, starting transfers between devices, per_device(): below = lax.ppermute(below, AXES, up)  5.75 us
    ppermute x3, starting transfers between devices, per_device(): below = lax.ppermute(below[below.shape[0] - last_rows(tiles):], AXES, up)  5.75 us
  transfers between devices with their start and end apart: 12, of which 7 were waited for; matrix products, arithmetic and copies ran while one was open for 0% of the time, Pallas kernels for 4%

profile of v1, /device:TPU:1, one launch (start us, length us, event | category | flops | bytes accessed | tf_op | source)
XLA Modules:
  0.0 129.6 jit_solution(15648088966068835324)
XLA Ops:
  0.0 1.1 copy-done.1
  1.1 0.7 copy-done.4
  1.8 0.9 shard_map.28.refs_3_.refs_6_
  2.7 14.2 %collective-permute-start.4 = (bf16[3088,128]{1,0:T(8,128)(2,1)S(1)}, bf16[3088,128]{1,0:T(8,128)(2,1)S(1)}, u32[]{:S(2)}, u32[]{:S(2)}) collective-permute-start(bf16[3088,128]{1,0:T(8,128)(2,1)S(1)} %shard_map.28.refs_3_.refs_6_), channel_id=1, source_target_pairs={{0,511},{1,0},{2,1},{3,2},{4,3},{5,4},{6,5},{7,6},{8,7},{9,8},{10,... | collective-permute-start | bytes 2371592 | tf_op jit(solution)/shard_map/ppermute | solution.py:288
  17.0 1.9 %collective-permute-start = (bf16[3088,128]{1,0:T(8,128)(2,1)S(1)}, bf16[3088,128]{1,0:T(8,128)(2,1)S(1)}, u32[]{:S(2)}, u32[]{:S(2)}) collective-permute-start(bf16[3088,128]{1,0:T(8,128)(2,1)S(1)} %shard_map.28.refs_3_.refs_6_), channel_id=1, source_target_pairs={{0,1},{1,2},{2,3},{3,4},{4,5},{5,6},{6,7},{7,8},{8,9},{9,10},{10,1... | collective-permute-start | bytes 2371592 | tf_op jit(solution)/shard_map/ppermute | solution.py:287
  18.9 15.5 %collective-permute-done.4.refs_4_.refs_7_ = bf16[3088,128]{1,0:T(8,128)(2,1)S(1)} collective-permute-done((bf16[3088,128]{1,0:T(8,128)(2,1)S(1)}, bf16[3088,128]{1,0:T(8,128)(2,1)S(1)}, u32[]{:S(2)}, u32[]{:S(2)}) %collective-permute-start.4) | collective-permute-done | bytes 790560 | tf_op jit(solution)/shard_map/ppermute | solution.py:288
  34.4 7.7 %collective-permute-start.5 = (bf16[3088,128]{1,0:T(8,128)(2,1)S(1)}, bf16[3088,128]{1,0:T(8,128)(2,1)S(1)}, u32[]{:S(2)}, u32[]{:S(2)}) collective-permute-start(bf16[3088,128]{1,0:T(8,128)(2,1)S(1)} %collective-permute-done.4.refs_4_.refs_7_), channel_id=1, source_target_pairs={{0,511},{1,0},{2,1},{3,2},{4,3},{5,4},{6,5},{7,6},{8,7},{9,8},{10,... | collective-permute-start | bytes 2371592 | tf_op jit(solution)/shard_map/ppermute | solution.py:288
  42.1 1.9 %collective-permute-start.1 = (bf16[3088,128]{1,0:T(8,128)(2,1)S(1)}, bf16[3088,128]{1,0:T(8,128)(2,1)S(1)}, u32[]{:S(2)}, u32[]{:S(2)}) collective-permute-start(bf16[3088,128]{1,0:T(8,128)(2,1)S(1)} %collective-permute-done.refs_2_.refs_5_), channel_id=1, source_target_pairs={{0,1},{1,2},{2,3},{3,4},{4,5},{5,6},{6,7},{7,8},{8,9},{9,10},{10,1... | collective-permute-start | bytes 2371592 | tf_op jit(solution)/shard_map/ppermute | solution.py:287
  44.1 9.7 %collective-permute-done.5.refs_5_.refs_8_ = bf16[3088,128]{1,0:T(8,128)(2,1)S(1)} collective-permute-done((bf16[3088,128]{1,0:T(8,128)(2,1)S(1)}, bf16[3088,128]{1,0:T(8,128)(2,1)S(1)}, u32[]{:S(2)}, u32[]{:S(2)}) %collective-permute-start.5) | collective-permute-done | bytes 790560 | tf_op jit(solution)/shard_map/ppermute | solution.py:288
  53.8 7.7 %collective-permute-start.6 = (bf16[3088,128]{1,0:T(8,128)(2,1)S(1)}, bf16[3088,128]{1,0:T(8,128)(2,1)S(1)}, u32[]{:S(2)}, u32[]{:S(2)}) collective-permute-start(bf16[3088,128]{1,0:T(8,128)(2,1)S(1)} %collective-permute-done.5.refs_5_.refs_8_), channel_id=1, source_target_pairs={{0,511},{1,0},{2,1},{3,2},{4,3},{5,4},{6,5},{7,6},{8,7},{9,8},{10,... | collective-permute-start | bytes 2371592 | tf_op jit(solution)/shard_map/ppermute | solution.py:288
  61.5 3.7 %collective-permute-done.1.refs_1_.refs_4_ = bf16[3088,128]{1,0:T(8,128)(2,1)S(1)} collective-permute-done((bf16[3088,128]{1,0:T(8,128)(2,1)S(1)}, bf16[3088,128]{1,0:T(8,128)(2,1)S(1)}, u32[]{:S(2)}, u32[]{:S(2)}) %collective-permute-start.1) | collective-permute-done | bytes 790560 | tf_op jit(solution)/shard_map/ppermute | solution.py:287
  65.2 1.9 %collective-permute-start.2 = (bf16[3088,128]{1,0:T(8,128)(2,1)S(1)}, bf16[3088,128]{1,0:T(8,128)(2,1)S(1)}, u32[]{:S(2)}, u32[]{:S(2)}) collective-permute-start(bf16[3088,128]{1,0:T(8,128)(2,1)S(1)} %collective-permute-done.1.refs_1_.refs_4_), channel_id=1, source_target_pairs={{0,1},{1,2},{2,3},{3,4},{4,5},{5,6},{6,7},{7,8},{8,9},{9,10},{10,1... | collective-permute-start | bytes 2371592 | tf_op jit(solution)/shard_map/ppermute | solution.py:287
  67.1 4.3 %collective-permute-done.6.refs_6_.refs_9_ = bf16[3088,128]{1,0:T(8,128)(2,1)S(1)} collective-permute-done((bf16[3088,128]{1,0:T(8,128)(2,1)S(1)}, bf16[3088,128]{1,0:T(8,128)(2,1)S(1)}, u32[]{:S(2)}, u32[]{:S(2)}) %collective-permute-start.6) | collective-permute-done | bytes 790560 | tf_op jit(solution)/shard_map/ppermute | solution.py:288
  71.5 7.7 %collective-permute-start.9 = (bf16[1344,128]{1,0:T(8,128)(2,1)S(1)}, bf16[1344,128]{1,0:T(8,128)(2,1)S(1)}, u32[]{:S(2)}, u32[]{:S(2)}) collective-permute-start(bf16[1344,128]{1,0:T(8,128)(2,1)S(1)} %slice.26), channel_id=1, source_target_pairs={{0,511},{1,0},{2,1},{3,2},{4,3},{5,4},{6,5},{7,6},{8,7},{9,8},{10,... | collective-permute-start | bytes 1032200 | tf_op jit(solution)/shard_map/ppermute | solution.py:296
  79.2 4.9 %collective-permute-done.2.refs_0_.refs_3_ = bf16[3088,128]{1,0:T(8,128)(2,1)S(1)} collective-permute-done((bf16[3088,128]{1,0:T(8,128)(2,1)S(1)}, bf16[3088,128]{1,0:T(8,128)(2,1)S(1)}, u32[]{:S(2)}, u32[]{:S(2)}) %collective-permute-start.2) | collective-permute-done | bytes 790560 | tf_op jit(solution)/shard_map/ppermute | solution.py:287
  84.1 1.9 %collective-permute-start.3 = (bf16[1216,128]{1,0:T(8,128)(2,1)S(1)}, bf16[1216,128]{1,0:T(8,128)(2,1)S(1)}, u32[]{:S(2)}, u32[]{:S(2)}) collective-permute-start(bf16[1216,128]{1,0:T(8,128)(2,1)S(1)} %slice.24), channel_id=1, source_target_pairs={{0,1},{1,2},{2,3},{3,4},{4,5},{5,6},{6,7},{7,8},{8,9},{9,10},{10,1... | collective-permute-start | bytes 933896 | tf_op jit(solution)/shard_map/ppermute | solution.py:295
  86.1 7.0 %collective-permute-start.10 = (bf16[832,128]{1,0:T(8,128)(2,1)S(1)}, bf16[832,128]{1,0:T(8,128)(2,1)S(1)}, u32[]{:S(2)}, u32[]{:S(2)}) collective-permute-start(bf16[832,128]{1,0:T(8,128)(2,1)S(1)} %slice.27), channel_id=1, source_target_pairs={{0,511},{1,0},{2,1},{3,2},{4,3},{5,4},{6,5},{7,6},{8,7},{9,8},{10,... | collective-permute-start | bytes 638984 | tf_op jit(solution)/shard_map/ppermute | solution.py:296
  93.0 5.5 %shard_map.29.refs_13_ = f32[256,1792]{1,0:T(8,128)} custom-call(bf16[3088,128]{1,0:T(8,128)(2,1)S(1)} %collective-permute-done.2.refs_0_.refs_3_, bf16[3088,128]{1,0:T(8,128)(2,1)S(1)} %collective-permute-done.1.refs_1_.refs_4_, bf16[3088,128]{1,0:T(8,128)(2,1)S(1)} %collective-permute-done.refs_2_.refs_5_, ...), custom_call_target="tpu_custom_call" | custom-call | flops 3758096384 | bytes 8388608 | tf_op jit(solution)/shard_map/pallas_call | solution.py:210
  98.6 1.9 %collective-permute-start.7 = (bf16[704,128]{1,0:T(8,128)(2,1)S(1)}, bf16[704,128]{1,0:T(8,128)(2,1)S(1)}, u32[]{:S(2)}, u32[]{:S(2)}) collective-permute-start(bf16[704,128]{1,0:T(8,128)(2,1)S(1)} %slice.19), channel_id=1, source_target_pairs={{0,1},{1,2},{2,3},{3,4},{4,5},{5,6},{6,7},{7,8},{8,9},{9,10},{10,1... | collective-permute-start | bytes 540680 | tf_op jit(solution)/shard_map/ppermute | solution.py:295
  100.6 7.0 %collective-permute-start.11 = (bf16[320,128]{1,0:T(8,128)(2,1)S(1)}, bf16[320,128]{1,0:T(8,128)(2,1)S(1)}, u32[]{:S(2)}, u32[]{:S(2)}) collective-permute-start(bf16[320,128]{1,0:T(8,128)(2,1)S(1)} %slice.28), channel_id=1, source_target_pairs={{0,511},{1,0},{2,1},{3,2},{4,3},{5,4},{6,5},{7,6},{8,7},{9,8},{10,... | collective-permute-start | bytes 245768 | tf_op jit(solution)/shard_map/ppermute | solution.py:296
  107.5 1.9 %collective-permute-done.7.refs_1_ = bf16[704,128]{1,0:T(8,128)(2,1)S(1)} collective-permute-done((bf16[704,128]{1,0:T(8,128)(2,1)S(1)}, bf16[704,128]{1,0:T(8,128)(2,1)S(1)}, u32[]{:S(2)}, u32[]{:S(2)}) %collective-permute-start.7) | collective-permute-done | bytes 180256 | tf_op jit(solution)/shard_map/ppermute | solution.py:295
  109.5 1.9 %collective-permute-start.8 = (bf16[192,128]{1,0:T(8,128)(2,1)S(1)}, bf16[192,128]{1,0:T(8,128)(2,1)S(1)}, u32[]{:S(2)}, u32[]{:S(2)}) collective-permute-start(bf16[192,128]{1,0:T(8,128)(2,1)S(1)} %slice.25), channel_id=1, source_target_pairs={{0,1},{1,2},{2,3},{3,4},{4,5},{5,6},{6,7},{7,8},{8,9},{9,10},{10,1... | collective-permute-start | bytes 147464 | tf_op jit(solution)/shard_map/ppermute | solution.py:295
  111.4 7.3 %collective-permute-done.8.refs_0_ = bf16[192,128]{1,0:T(8,128)(2,1)S(1)} collective-permute-done((bf16[192,128]{1,0:T(8,128)(2,1)S(1)}, bf16[192,128]{1,0:T(8,128)(2,1)S(1)}, u32[]{:S(2)}, u32[]{:S(2)}) %collective-permute-start.8) | collective-permute-done | bytes 49184 | tf_op jit(solution)/shard_map/ppermute | solution.py:295
  120.0 9.6 %shard_map.30 = bf16[4,64,1536]{2,1,0:T(8,128)(2,1)} custom-call(bf16[192,128]{1,0:T(8,128)(2,1)} %copy-done.14, bf16[704,128]{1,0:T(8,128)(2,1)} %copy-done.12, bf16[1216,128]{1,0:T(8,128)(2,1)} %copy-done.10, bf16[3088,128]{1,0:T(8,128)(2,1)} %copy-done.3, bf16[3088,128]{1,0:T(8,128)(2,1)} %copy-done.8, bf16[3088,128]{1,0:T(8,128)(2,1)} %copy-done.6, ...), custom_call_target="tpu_custom_call" | custom-call | flops 4294967296 | bytes 12582912 | tf_op jit(solution)/shard_map/pallas_call | solution.py:265
  (39 shorter events, 1.4 us)
Async XLA Ops:
  0.0 1.1 copy-start.1
  2.7 95.8 %copy-start = (bf16[3088,128]{1,0:T(8,128)(2,1)}, bf16[3088,128]{1,0:T(8,128)(2,1)S(1)}, u32[]{:S(2)}) copy-start(bf16[3088,128]{1,0:T(8,128)(2,1)S(1)} %shard_map.28.refs_3_.refs_6_) | copy-start | bytes 2371588
  2.7 31.7 %collective-permute-start.4 = (bf16[3088,128]{1,0:T(8,128)(2,1)S(1)}, bf16[3088,128]{1,0:T(8,128)(2,1)S(1)}, u32[]{:S(2)}, u32[]{:S(2)}) collective-permute-start(bf16[3088,128]{1,0:T(8,128)(2,1)S(1)} %shard_map.28.refs_3_.refs_6_), channel_id=1, source_target_pairs={{0,511},{1,0},{2,1},{3,2},{4,3},{5,4},{6,5},{7,6},{8,7},{9,8},{10,... | collective-permute-start | bytes 2371592 | tf_op jit(solution)/shard_map/ppermute | solution.py:288
  17.0 25.1 %collective-permute-start = (bf16[3088,128]{1,0:T(8,128)(2,1)S(1)}, bf16[3088,128]{1,0:T(8,128)(2,1)S(1)}, u32[]{:S(2)}, u32[]{:S(2)}) collective-permute-start(bf16[3088,128]{1,0:T(8,128)(2,1)S(1)} %shard_map.28.refs_3_.refs_6_), channel_id=1, source_target_pairs={{0,1},{1,2},{2,3},{3,4},{4,5},{5,6},{6,7},{7,8},{8,9},{9,10},{10,1... | collective-permute-start | bytes 2371592 | tf_op jit(solution)/shard_map/ppermute | solution.py:287
  34.4 64.1 %copy-start.5 = (bf16[3088,128]{1,0:T(8,128)(2,1)}, bf16[3088,128]{1,0:T(8,128)(2,1)S(1)}, u32[]{:S(2)}) copy-start(bf16[3088,128]{1,0:T(8,128)(2,1)S(1)} %collective-permute-done.4.refs_4_.refs_7_) | copy-start | bytes 2371588
  34.4 19.4 %collective-permute-start.5 = (bf16[3088,128]{1,0:T(8,128)(2,1)S(1)}, bf16[3088,128]{1,0:T(8,128)(2,1)S(1)}, u32[]{:S(2)}, u32[]{:S(2)}) collective-permute-start(bf16[3088,128]{1,0:T(8,128)(2,1)S(1)} %collective-permute-done.4.refs_4_.refs_7_), channel_id=1, source_target_pairs={{0,511},{1,0},{2,1},{3,2},{4,3},{5,4},{6,5},{7,6},{8,7},{9,8},{10,... | collective-permute-start | bytes 2371592 | tf_op jit(solution)/shard_map/ppermute | solution.py:288
  42.1 56.4 %copy-start.6 = (bf16[3088,128]{1,0:T(8,128)(2,1)}, bf16[3088,128]{1,0:T(8,128)(2,1)S(1)}, u32[]{:S(2)}) copy-start(bf16[3088,128]{1,0:T(8,128)(2,1)S(1)} %collective-permute-done.refs_2_.refs_5_) | copy-start | bytes 2371588
  42.1 23.0 %collective-permute-start.1 = (bf16[3088,128]{1,0:T(8,128)(2,1)S(1)}, bf16[3088,128]{1,0:T(8,128)(2,1)S(1)}, u32[]{:S(2)}, u32[]{:S(2)}) collective-permute-start(bf16[3088,128]{1,0:T(8,128)(2,1)S(1)} %collective-permute-done.refs_2_.refs_5_), channel_id=1, source_target_pairs={{0,1},{1,2},{2,3},{3,4},{4,5},{5,6},{6,7},{7,8},{8,9},{9,10},{10,1... | collective-permute-start | bytes 2371592 | tf_op jit(solution)/shard_map/ppermute | solution.py:287
  53.8 44.7 %copy-start.7 = (bf16[3088,128]{1,0:T(8,128)(2,1)}, bf16[3088,128]{1,0:T(8,128)(2,1)S(1)}, u32[]{:S(2)}) copy-start(bf16[3088,128]{1,0:T(8,128)(2,1)S(1)} %collective-permute-done.5.refs_5_.refs_8_) | copy-start | bytes 2371588
  53.8 17.7 %collective-permute-start.6 = (bf16[3088,128]{1,0:T(8,128)(2,1)S(1)}, bf16[3088,128]{1,0:T(8,128)(2,1)S(1)}, u32[]{:S(2)}, u32[]{:S(2)}) collective-permute-start(bf16[3088,128]{1,0:T(8,128)(2,1)S(1)} %collective-permute-done.5.refs_5_.refs_8_), channel_id=1, source_target_pairs={{0,511},{1,0},{2,1},{3,2},{4,3},{5,4},{6,5},{7,6},{8,7},{9,8},{10,... | collective-permute-start | bytes 2371592 | tf_op jit(solution)/shard_map/ppermute | solution.py:288
  65.2 33.3 %copy-start.8 = (bf16[3088,128]{1,0:T(8,128)(2,1)}, bf16[3088,128]{1,0:T(8,128)(2,1)S(1)}, u32[]{:S(2)}) copy-start(bf16[3088,128]{1,0:T(8,128)(2,1)S(1)} %collective-permute-done.1.refs_1_.refs_4_) | copy-start | bytes 2371588
  65.2 18.9 %collective-permute-start.2 = (bf16[3088,128]{1,0:T(8,128)(2,1)S(1)}, bf16[3088,128]{1,0:T(8,128)(2,1)S(1)}, u32[]{:S(2)}, u32[]{:S(2)}) collective-permute-start(bf16[3088,128]{1,0:T(8,128)(2,1)S(1)} %collective-permute-done.1.refs_1_.refs_4_), channel_id=1, source_target_pairs={{0,1},{1,2},{2,3},{3,4},{4,5},{5,6},{6,7},{7,8},{8,9},{9,10},{10,1... | collective-permute-start | bytes 2371592 | tf_op jit(solution)/shard_map/ppermute | solution.py:287
  71.4 27.1 %copy-start.2 = (bf16[3088,128]{1,0:T(8,128)(2,1)}, bf16[3088,128]{1,0:T(8,128)(2,1)S(1)}, u32[]{:S(2)}) copy-start(bf16[3088,128]{1,0:T(8,128)(2,1)S(1)} %collective-permute-done.6.refs_6_.refs_9_) | copy-start | bytes 2371588
  71.5 14.5 %collective-permute-start.9 = (bf16[1344,128]{1,0:T(8,128)(2,1)S(1)}, bf16[1344,128]{1,0:T(8,128)(2,1)S(1)}, u32[]{:S(2)}, u32[]{:S(2)}) collective-permute-start(bf16[1344,128]{1,0:T(8,128)(2,1)S(1)} %slice.26), channel_id=1, source_target_pairs={{0,511},{1,0},{2,1},{3,2},{4,3},{5,4},{6,5},{7,6},{8,7},{9,8},{10,... | collective-permute-start | bytes 1032200 | tf_op jit(solution)/shard_map/ppermute | solution.py:296
  84.1 14.5 %copy-start.3 = (bf16[3088,128]{1,0:T(8,128)(2,1)}, bf16[3088,128]{1,0:T(8,128)(2,1)S(1)}, u32[]{:S(2)}) copy-start(bf16[3088,128]{1,0:T(8,128)(2,1)S(1)} %collective-permute-done.2.refs_0_.refs_3_) | copy-start | bytes 2371588
  84.1 14.5 %collective-permute-start.3 = (bf16[1216,128]{1,0:T(8,128)(2,1)S(1)}, bf16[1216,128]{1,0:T(8,128)(2,1)S(1)}, u32[]{:S(2)}, u32[]{:S(2)}) collective-permute-start(bf16[1216,128]{1,0:T(8,128)(2,1)S(1)} %slice.24), channel_id=1, source_target_pairs={{0,1},{1,2},{2,3},{3,4},{4,5},{5,6},{6,7},{7,8},{8,9},{9,10},{10,1... | collective-permute-start | bytes 933896 | tf_op jit(solution)/shard_map/ppermute | solution.py:295
  86.0 12.5 %copy-start.9 = (bf16[1344,128]{1,0:T(8,128)(2,1)}, bf16[1344,128]{1,0:T(8,128)(2,1)S(1)}, u32[]{:S(2)}) copy-start(bf16[1344,128]{1,0:T(8,128)(2,1)S(1)} %collective-permute-done.9.refs_10_) | copy-start | bytes 1032196
  86.1 14.5 %collective-permute-start.10 = (bf16[832,128]{1,0:T(8,128)(2,1)S(1)}, bf16[832,128]{1,0:T(8,128)(2,1)S(1)}, u32[]{:S(2)}, u32[]{:S(2)}) collective-permute-start(bf16[832,128]{1,0:T(8,128)(2,1)S(1)} %slice.27), channel_id=1, source_target_pairs={{0,511},{1,0},{2,1},{3,2},{4,3},{5,4},{6,5},{7,6},{8,7},{9,8},{10,... | collective-permute-start | bytes 638984 | tf_op jit(solution)/shard_map/ppermute | solution.py:296
  98.6 20.2 %copy-start.10 = (bf16[1216,128]{1,0:T(8,128)(2,1)}, bf16[1216,128]{1,0:T(8,128)(2,1)S(1)}, u32[]{:S(2)}) copy-start(bf16[1216,128]{1,0:T(8,128)(2,1)S(1)} %collective-permute-done.3.refs_2_) | copy-start | bytes 933892
  98.6 10.9 %collective-permute-start.7 = (bf16[704,128]{1,0:T(8,128)(2,1)S(1)}, bf16[704,128]{1,0:T(8,128)(2,1)S(1)}, u32[]{:S(2)}, u32[]{:S(2)}) collective-permute-start(bf16[704,128]{1,0:T(8,128)(2,1)S(1)} %slice.19), channel_id=1, source_target_pairs={{0,1},{1,2},{2,3},{3,4},{4,5},{5,6},{6,7},{7,8},{8,9},{9,10},{10,1... | collective-permute-start | bytes 540680 | tf_op jit(solution)/shard_map/ppermute | solution.py:295
  100.5 18.2 %copy-start.11 = (bf16[832,128]{1,0:T(8,128)(2,1)}, bf16[832,128]{1,0:T(8,128)(2,1)S(1)}, u32[]{:S(2)}) copy-start(bf16[832,128]{1,0:T(8,128)(2,1)S(1)} %collective-permute-done.10.refs_11_) | copy-start | bytes 638980
  100.6 18.2 %collective-permute-start.11 = (bf16[320,128]{1,0:T(8,128)(2,1)S(1)}, bf16[320,128]{1,0:T(8,128)(2,1)S(1)}, u32[]{:S(2)}, u32[]{:S(2)}) collective-permute-start(bf16[320,128]{1,0:T(8,128)(2,1)S(1)} %slice.28), channel_id=1, source_target_pairs={{0,511},{1,0},{2,1},{3,2},{4,3},{5,4},{6,5},{7,6},{8,7},{9,8},{10,... | collective-permute-start | bytes 245768 | tf_op jit(solution)/shard_map/ppermute | solution.py:296
  109.5 9.3 %copy-start.12 = (bf16[704,128]{1,0:T(8,128)(2,1)}, bf16[704,128]{1,0:T(8,128)(2,1)S(1)}, u32[]{:S(2)}) copy-start(bf16[704,128]{1,0:T(8,128)(2,1)S(1)} %collective-permute-done.7.refs_1_) | copy-start | bytes 540676
  109.5 9.3 %collective-permute-start.8 = (bf16[192,128]{1,0:T(8,128)(2,1)S(1)}, bf16[192,128]{1,0:T(8,128)(2,1)S(1)}, u32[]{:S(2)}, u32[]{:S(2)}) collective-permute-start(bf16[192,128]{1,0:T(8,128)(2,1)S(1)} %slice.25), channel_id=1, source_target_pairs={{0,1},{1,2},{2,3},{3,4},{4,5},{5,6},{6,7},{7,8},{8,9},{9,10},{10,1... | collective-permute-start | bytes 147464 | tf_op jit(solution)/shard_map/ppermute | solution.py:295
  (3 other events, 1.9 us)

commit v2 on v1

v2 whole, which is shorter than its diff:
```python
import functools

import jax
import jax.numpy as jnp
from jax import lax
from jax.experimental import pallas as pl
from jax.experimental.pallas import tpu as pltpu
from jax.sharding import PartitionSpec as P

AXES = ("row", "col")
BLOCK = 64
ROWS = 4
TILE = ROWS * BLOCK
REACH = 3
TILES = 2 * REACH + 1
HEAD = 5 * BLOCK
BODY = 10 * TILE
TAIL = 3 * BLOCK
DATA = HEAD + BODY + TAIL
NOTE = 16
ALL = NOTE + DATA + NOTE
F32 = jnp.float32
BF16 = jnp.bfloat16
VMEM = pl.BlockSpec(memory_space=pltpu.VMEM)
SMEM = pl.BlockSpec(memory_space=pltpu.SMEM)


def first_rows(tiles):
    return HEAD + (tiles - 1) * 2 * TILE


def last_rows(tiles):
    return TAIL + (tiles - 1) * 2 * TILE


def half_lanes(rows):
    return lax.broadcasted_iota(jnp.int32, (rows, 128), 1) < BLOCK


def swap_halves(piece):
    return pltpu.roll(piece.astype(F32), BLOCK, 1)


def pack_kernel(x_ref, pattern_ref, out_ref):
    low = half_lanes(BLOCK)
    zero = jnp.zeros((BLOCK, 128), F32)
    note = jnp.zeros((NOTE, 128), F32)
    lane = lax.broadcasted_iota(jnp.int32, (NOTE, 128), 1)
    row = lax.broadcasted_iota(jnp.int32, (NOTE, 128), 0)
    slots = x_ref.shape[2] // BLOCK
    strips = []
    for q in range(ROWS):
        pieces = []
        for pair in range(slots // 2):
            even = pattern_ref[q, 2 * pair]
            odd = pattern_ref[q, 2 * pair + 1]
            keep = jnp.where(low, even, odd) == 1
            piece = x_ref[q, :, pair * 128 : (pair + 1) * 128].astype(F32)
            pieces.append(jnp.where(keep, piece, 0.0))
            for slot, present in ((2 * pair, even), (2 * pair + 1, odd)):
                value = jnp.where(present == 1, 1.0, 0.0)
                note = jnp.where((row == q) & (lane == slot + q), value, note)
        shifted = [zero] * (q // 2)
        if q % 2 == 0:
            shifted += pieces
        else:
            turned = [swap_halves(piece) for piece in pieces]
            shifted.append(jnp.where(low, 0.0, turned[0]))
            for left, right in zip(turned[:-1], turned[1:]):
                shifted.append(jnp.where(low, left, right))
            shifted.append(jnp.where(low, turned[-1], 0.0))
        shifted += [zero] * (2 * TILES - len(shifted))
        strips.append(shifted)

    def put(start, piece):
        out_ref[NOTE + start : NOTE + start + BLOCK, :] = piece.astype(BF16)

    put(0, strips[0][0])
    put(BLOCK, strips[0][1])
    put(2 * BLOCK, strips[1][1])
    put(3 * BLOCK, strips[2][1])
    put(4 * BLOCK, jnp.where(low, swap_halves(strips[3][1]), strips[1][0]))
    for pair in range(2, 2 * TILES - 2):
        for q in range(ROWS):
            put(HEAD + (pair - 2) * TILE + q * BLOCK, strips[q][pair])
    put(HEAD + BODY, strips[2][2 * TILES - 2])
    put(HEAD + BODY + BLOCK, strips[3][2 * TILES - 2])
    put(
        HEAD + BODY + 2 * BLOCK,
        jnp.where(low, strips[1][2 * TILES - 2], swap_halves(strips[3][2 * TILES - 1])),
    )
    out_ref[:NOTE, :] = note.astype(BF16)
    out_ref[NOTE + DATA :, :] = note.astype(BF16)


def pack(x, pattern):
    return pl.pallas_call(
        pack_kernel,
        out_shape=jax.ShapeDtypeStruct((ALL, 128), BF16),
        in_specs=[VMEM, SMEM],
        out_specs=VMEM,
        compiler_params=pltpu.CompilerParams(vmem_limit_bytes=32 << 20),
        cost_estimate=pl.CostEstimate(flops=1 << 20, bytes_accessed=3 << 20, transcendentals=0),
    )(x, pattern)


def unpack_tile(source, tile, base, window, row, col):
    def put(q, half, piece):
        window[pl.ds(row + q * BLOCK, BLOCK), pl.ds(col + half * 128, 128)] = piece

    low = half_lanes(BLOCK)
    zero = jnp.zeros((BLOCK, 128), BF16)
    if tile == 0:

        def seg(k):
            return source[base + k * BLOCK : base + (k + 1) * BLOCK, :]

        mixed = seg(4)
        put(0, 0, seg(0))
        put(0, 1, seg(1))
        put(1, 0, jnp.where(low, 0.0, mixed.astype(F32)).astype(BF16))
        put(1, 1, seg(2))
        put(2, 0, zero)
        put(2, 1, seg(3))
        put(3, 0, zero)
        put(3, 1, jnp.where(low, 0.0, swap_halves(mixed)).astype(BF16))
    elif tile == TILES - 1:

        def seg(k):
            return source[base + k * BLOCK : base + (k + 1) * BLOCK, :]

        mixed = seg(2)
        put(0, 0, zero)
        put(0, 1, zero)
        put(1, 0, jnp.where(low, mixed.astype(F32), 0.0).astype(BF16))
        put(1, 1, zero)
        put(2, 0, seg(0))
        put(2, 1, zero)
        put(3, 0, seg(1))
        put(3, 1, jnp.where(low, swap_halves(mixed), 0.0).astype(BF16))
    else:
        for half in range(2):
            start = base + half * TILE
            window[row : row + TILE, col + half * 128 : col + half * 128 + 128] = source[start : start + TILE, :]


def tile_start(tile, first):
    def whole(t):
        return 0 if t == 0 else HEAD + (t - 1) * 2 * TILE

    return whole(tile) - whole(first)


def spread(note):
    lane = lax.broadcasted_iota(jnp.int32, (128, TILES * TILE), 1) // BLOCK
    block = lax.broadcasted_iota(jnp.int32, (128, TILES * TILE), 0)
    return jnp.dot(note, jnp.where(lane == block, 1.0, 0.0).astype(BF16), preferred_element_type=F32)


def square_tiles(jobs, window, notes, square):
    for k, c, first, last in jobs:
        depth = slice((first + REACH) * TILE, (last + REACH + 1) * TILE)
        total = jnp.dot(
            window[(k + REACH) * TILE : (k + REACH + 1) * TILE, depth],
            window[depth, (c + REACH) * TILE : (c + REACH + 1) * TILE],
            preferred_element_type=F32,
        )
        place = (c - k + REACH) * TILE
        for q in range(ROWS):
            keep = notes[k][q : q + 1, place : place + TILE] > 0.5
            square[
                pl.ds((k + REACH) * TILE + q * BLOCK, BLOCK), pl.ds((c + REACH) * TILE, TILE)
            ] = jnp.where(keep, total[q * BLOCK : (q + 1) * BLOCK], 0.0).astype(BF16)


SPAN = range(-REACH, REACH + 1)
OWN_JOBS = [
    (k, c, max(k, c, 0) - REACH, min(k, c, 0) + REACH) for k in SPAN for c in SPAN if abs(k - c) <= REACH
]
UP_JOBS = [(k, c, max(k, c) - REACH, -1) for k in range(REACH) for c in range(REACH)]
DOWN_JOBS = [(-k, -c, 1, REACH - max(k, c)) for k in range(REACH) for c in range(REACH)]


def needed(jobs):
    return {t for k, c, first, last in jobs for l in range(first, last + 1) for t in ((k, l), (l, c))}


def load_window(refs, tiles, window):
    for r, t in sorted(tiles):
        j = t - r + REACH
        first = max(-r, 0)
        base = 0 if r < 0 else NOTE
        unpack_tile(
            refs[r + REACH],
            j,
            base + tile_start(j, first),
            window,
            (r + REACH) * TILE,
            (t + REACH) * TILE,
        )


def load_notes(refs, rows):
    return {
        k: spread(refs[k + REACH][-NOTE:, :] if k < 0 else refs[k + REACH][:NOTE, :]) for k in rows
    }


def pack_tile(total, tile, first, out_ref):
    base = tile_start(tile, first)
    low = half_lanes(BLOCK)

    def piece(q, half):
        return total[q * BLOCK : (q + 1) * BLOCK, half * 128 : half * 128 + 128]

    def put(k, value):
        out_ref[base + k * BLOCK : base + (k + 1) * BLOCK, :] = value.astype(BF16)

    if tile == 0:
        put(0, piece(0, 0))
        put(1, piece(0, 1))
        put(2, piece(1, 1))
        put(3, piece(2, 1))
        put(4, jnp.where(low, swap_halves(piece(3, 1)), piece(1, 0)))
    elif tile == TILES - 1:
        put(0, piece(2, 0))
        put(1, piece(3, 0))
        put(2, jnp.where(low, piece(1, 0), swap_halves(piece(3, 1))))
    else:
        for half in range(2):
            for q in range(ROWS):
                put(half * ROWS + q, piece(q, half))


def tile_rows(k):
    return slice((k + REACH) * TILE, (k + REACH + 1) * TILE)


def edge_kernel(*refs):
    up_ref, down_ref, window, square = refs[TILES:]
    outer = {(REACH, k) for k in range(REACH)} | {(-REACH, -k) for k in range(REACH)}
    load_window(refs, needed(UP_JOBS) | needed(DOWN_JOBS) | outer, window)
    notes = load_notes(refs, range(1 - REACH, REACH))
    for jobs, row, cols, shift, first, out_ref in (
        (UP_JOBS, REACH, range(REACH), 0, 0, up_ref),
        (DOWN_JOBS, -REACH, range(1 - REACH, 1), 2 * REACH, REACH + 1, down_ref),
    ):
        square_tiles(jobs, window, notes, square)
        depth = slice((cols[0] + REACH) * TILE, (cols[-1] + REACH + 1) * TILE)
        for c in cols:
            total = jnp.dot(
                window[tile_rows(row), depth], square[depth, tile_rows(c)], preferred_element_type=F32
            )
            pack_tile(total, c + shift, first, out_ref)


def own_kernel(*refs):
    out_ref, window, square = refs[TILES:]
    load_window(refs, needed(OWN_JOBS), window)
    square_tiles(OWN_JOBS, window, load_notes(refs, SPAN), square)
    for c in SPAN:
        depth = slice(max(c, 0) * TILE, (min(c, 0) + TILES) * TILE)
        total = jnp.dot(window[tile_rows(0), depth], square[depth, tile_rows(c)], preferred_element_type=F32)
        x = window[tile_rows(0), tile_rows(c)].astype(F32)
        out_ref[:, tile_rows(c)] = 1.5 * x - 0.5 * total


def window_call(kernel, products, out_shape, messages):
    return pl.pallas_call(
        kernel,
        out_shape=out_shape,
        in_specs=[VMEM] * TILES,
        out_specs=jax.tree.map(lambda _: VMEM, out_shape),
        scratch_shapes=[
            pltpu.VMEM((TILES * TILE, TILES * TILE), BF16),
            pltpu.VMEM((TILES * TILE, TILES * TILE), BF16),
        ],
        compiler_params=pltpu.CompilerParams(vmem_limit_bytes=48 << 20),
        cost_estimate=pl.CostEstimate(
            flops=products * 2 * TILE**3, bytes_accessed=6 << 20, transcendentals=0
        ),
    )(*messages)


def finish_kernel(part_ref, up_ref, down_ref, note_ref, out_ref, extra):
    for tile in range(REACH):
        unpack_tile(up_ref, tile, tile_start(tile, 0), extra, 0, tile * TILE)
        far = REACH + 1 + tile
        unpack_tile(down_ref, far, tile_start(far, REACH + 1), extra, 0, (REACH + tile) * TILE)
    keep = spread(note_ref[:NOTE, :])
    width = out_ref.shape[2]
    side = REACH * TILE
    for q in range(ROWS):
        rows = slice(q * BLOCK, (q + 1) * BLOCK)
        more = extra[rows, :].astype(F32)
        strip = jnp.concatenate(
            [
                part_ref[rows, :side] - 0.5 * more[:, :side],
                part_ref[rows, side : side + TILE],
                part_ref[rows, side + TILE :] - 0.5 * more[:, side:],
            ],
            axis=1,
        )
        strip = jnp.where(keep[q : q + 1] > 0.5, strip, 0.0)
        if q % 2:
            strip = pltpu.roll(strip, TILES * TILE - BLOCK, 1)
        start = (q // 2) * 128
        out_ref[q] = strip[:, start : start + width].astype(BF16)


def finish(part, up, down, own, out_type):
    return pl.pallas_call(
        finish_kernel,
        out_shape=out_type,
        in_specs=[VMEM] * 4,
        out_specs=VMEM,
        scratch_shapes=[pltpu.VMEM((TILE, 2 * REACH * TILE), BF16)],
        compiler_params=pltpu.CompilerParams(vmem_limit_bytes=32 << 20),
        cost_estimate=pl.CostEstimate(flops=4 << 20, bytes_accessed=4 << 20, transcendentals=0),
    )(part, up, down, own)


def per_device(count, x, pattern):
    def shift(steps):
        return [(n, (n + steps) % count) for n in range(count)]

    own = pack(x, pattern)
    held = {0: own}
    below = own
    above = own
    for step in range(1, REACH + 1):
        tiles = TILES - step
        below = lax.ppermute(below[below.shape[0] - NOTE - last_rows(tiles) :], AXES, shift(1))
        above = lax.ppermute(above[: NOTE + first_rows(tiles)], AXES, shift(-1))
        held[-step], held[step] = below, above
    messages = [held[k] for k in SPAN]
    up, down = window_call(
        edge_kernel,
        46,
        (
            jax.ShapeDtypeStruct((first_rows(REACH), 128), BF16),
            jax.ShapeDtypeStruct((last_rows(REACH), 128), BF16),
        ),
        messages,
    )
    part = window_call(own_kernel, 212, jax.ShapeDtypeStruct((TILE, TILES * TILE), F32), messages)
    up = lax.ppermute(up, AXES, shift(REACH))
    down = lax.ppermute(down, AXES, shift(-REACH))
    return finish(part, up, down, own, jax.ShapeDtypeStruct(x.shape, x.dtype))


def solution(mesh):
    placed = (P(AXES, None, None), P(AXES, None))
    count = mesh.shape["row"] * mesh.shape["col"]
    return jax.shard_map(
        functools.partial(per_device, count),
        mesh=mesh,
        in_specs=placed,
        out_specs=P(AXES, None, None),
        check_vma=False,
    )
```

time: 130 us -> 104 us (0.80)
  starting transfers between devices: 62.8 us -> 46.1 us
  waiting for transfers between devices: 47.4 us -> 43.1 us
  Pallas kernels: 16 us -> 12.3 us
    ppermute x12 -> x8, starting transfers between devices: 62.8 us -> 46.1 us  [the longest x3 29.7 us: per_device(): above = lax.ppermute(above[:NOTE + first_rows(tiles)], AXES, shift(-1))]
    ppermute x12 -> x8, waiting for transfers between devices: 47.4 us -> 43.1 us  [the longest x3 20.2 us: per_device(): above = lax.ppermute(above[:NOTE + first_rows(tiles)], AXES, shift(-1))]
    pallas_call x2 -> x3, Pallas kernels: 15.1 us -> 11.4 us  [the longest x2 10 us: window_call(): pl.pallas_call(kernel, out_shape=out_shape, in_specs=[VMEM] * TILES, out_...]
    unnamed x30 -> x4, local copies, waits for them, and re-layouts: 3.07 us -> 1.81 us
  transfers between devices with their start and end apart: 12 -> 8, of which waited for: 7 -> 5; matrix products, arithmetic and copies ran while one was open for 0% -> 0% of each run, Pallas kernels for 4% -> 7%
where the time goes in v2:
time: 104 us
  starting transfers between devices  46.1 us (44%)
  waiting for transfers between devices  43.1 us (41%)
  Pallas kernels  12.3 us (12%)
  local copies, waits for them, and re-layouts  2.05 us (2%)
    ppermute x3, starting transfers between devices, per_device(): above = lax.ppermute(above[:NOTE + first_rows(tiles)], AXES, shift(-1))  29.7 us
    ppermute x3, waiting for transfers between devices, per_device(): above = lax.ppermute(above[:NOTE + first_rows(tiles)], AXES, shift(-1))  20.2 us
    ppermute x3, waiting for transfers between devices, per_device(): lax.ppermute(below[below.shape[0] - NOTE - last_rows(tiles):], AXES, shif...  15.7 us
    pallas_call x2, Pallas kernels, window_call(): pl.pallas_call(kernel, out_shape=out_shape, in_specs=[VMEM] * TILES, out_...  10 us
    ppermute x1, starting transfers between devices, per_device(): down = lax.ppermute(down, AXES, shift(-REACH))  8.76 us
    ppermute x1, waiting for transfers between devices, per_device(): down = lax.ppermute(down, AXES, shift(-REACH))  7.12 us
    ppermute x3, starting transfers between devices, per_device(): lax.ppermute(below[below.shape[0] - NOTE - last_rows(tiles):], AXES, shif...  5.76 us
  transfers between devices with their start and end apart: 8, of which 5 were waited for; matrix products, arithmetic and copies ran while one was open for 0% of the time, Pallas kernels for 7%

profile of v2, /device:TPU:1, one launch (start us, length us, event | category | flops | bytes accessed | tf_op | source)
XLA Modules:
  0.0 103.6 jit_solution(16786159590397191490)
XLA Ops:
  0.0 0.0 copy-start
  0.0 1.1 %copy-done = bf16[4,64,1536]{2,1,0:T(8,128)(2,1)S(1)} copy-done((bf16[4,64,1536]{2,1,0:T(8,128)(2,1)S(1)}, bf16[4,64,1536]{2,1,0:T(8,128)(2,1)}, u32[]{:S(2)}) %copy-start) | copy-done | bytes 786456
  1.1 0.0 copy-start.1
  1.1 0.7 copy-done.1
  1.8 0.9 shard_map.28.refs_3_.note_ref
  2.8 14.3 %collective-permute-start.3 = (bf16[2896,128]{1,0:T(8,128)(2,1)S(1)}, bf16[2896,128]{1,0:T(8,128)(2,1)S(1)}, u32[]{:S(2)}, u32[]{:S(2)}) collective-permute-start(bf16[2896,128]{1,0:T(8,128)(2,1)S(1)} %slice.27), channel_id=1, source_target_pairs={{0,511},{1,0},{2,1},{3,2},{4,3},{5,4},{6,5},{7,6},{8,7},{9,8},{10,... | collective-permute-start | bytes 2224136 | tf_op jit(solution)/shard_map/ppermute | solution.py:334
  17.1 1.9 %collective-permute-start = (bf16[2768,128]{1,0:T(8,128)(2,1)S(1)}, bf16[2768,128]{1,0:T(8,128)(2,1)S(1)}, u32[]{:S(2)}, u32[]{:S(2)}) collective-permute-start(bf16[2768,128]{1,0:T(8,128)(2,1)S(1)} %slice.24), channel_id=1, source_target_pairs={{0,1},{1,2},{2,3},{3,4},{4,5},{5,6},{6,7},{7,8},{8,9},{9,10},{10,1... | collective-permute-start | bytes 2125832 | tf_op jit(solution)/shard_map/ppermute | solution.py:333
  19.0 14.4 %collective-permute-done.3.refs_4_ = bf16[2896,128]{1,0:T(8,128)(2,1)S(1)} collective-permute-done((bf16[2896,128]{1,0:T(8,128)(2,1)S(1)}, bf16[2896,128]{1,0:T(8,128)(2,1)S(1)}, u32[]{:S(2)}, u32[]{:S(2)}) %collective-permute-start.3) | collective-permute-done | bytes 741408 | tf_op jit(solution)/shard_map/ppermute | solution.py:334
  33.5 7.7 %collective-permute-start.4 = (bf16[2384,128]{1,0:T(8,128)(2,1)S(1)}, bf16[2384,128]{1,0:T(8,128)(2,1)S(1)}, u32[]{:S(2)}, u32[]{:S(2)}) collective-permute-start(bf16[2384,128]{1,0:T(8,128)(2,1)S(1)} %slice.28), channel_id=1, source_target_pairs={{0,511},{1,0},{2,1},{3,2},{4,3},{5,4},{6,5},{7,6},{8,7},{9,8},{10,... | collective-permute-start | bytes 1830920 | tf_op jit(solution)/shard_map/ppermute | solution.py:334
  41.2 0.0 collective-permute-done.refs_2_
  41.2 1.9 %collective-permute-start.1 = (bf16[2256,128]{1,0:T(8,128)(2,1)S(1)}, bf16[2256,128]{1,0:T(8,128)(2,1)S(1)}, u32[]{:S(2)}, u32[]{:S(2)}) collective-permute-start(bf16[2256,128]{1,0:T(8,128)(2,1)S(1)} %slice.25), channel_id=1, source_target_pairs={{0,1},{1,2},{2,3},{3,4},{4,5},{5,6},{6,7},{7,8},{8,9},{9,10},{10,1... | collective-permute-start | bytes 1732616 | tf_op jit(solution)/shard_map/ppermute | solution.py:333
  43.2 5.8 %collective-permute-done.4.refs_5_ = bf16[2384,128]{1,0:T(8,128)(2,1)S(1)} collective-permute-done((bf16[2384,128]{1,0:T(8,128)(2,1)S(1)}, bf16[2384,128]{1,0:T(8,128)(2,1)S(1)}, u32[]{:S(2)}, u32[]{:S(2)}) %collective-permute-start.4) | collective-permute-done | bytes 610336 | tf_op jit(solution)/shard_map/ppermute | solution.py:334
  49.0 7.7 %collective-permute-start.5 = (bf16[1872,128]{1,0:T(8,128)(2,1)S(1)}, bf16[1872,128]{1,0:T(8,128)(2,1)S(1)}, u32[]{:S(2)}, u32[]{:S(2)}) collective-permute-start(bf16[1872,128]{1,0:T(8,128)(2,1)S(1)} %slice.29), channel_id=1, source_target_pairs={{0,511},{1,0},{2,1},{3,2},{4,3},{5,4},{6,5},{7,6},{8,7},{9,8},{10,... | collective-permute-start | bytes 1437704 | tf_op jit(solution)/shard_map/ppermute | solution.py:334
  56.7 3.5 %collective-permute-done.1.refs_1_ = bf16[2256,128]{1,0:T(8,128)(2,1)S(1)} collective-permute-done((bf16[2256,128]{1,0:T(8,128)(2,1)S(1)}, bf16[2256,128]{1,0:T(8,128)(2,1)S(1)}, u32[]{:S(2)}, u32[]{:S(2)}) %collective-permute-start.1) | collective-permute-done | bytes 577568 | tf_op jit(solution)/shard_map/ppermute | solution.py:333
  60.3 1.9 %collective-permute-start.2 = (bf16[1744,128]{1,0:T(8,128)(2,1)S(1)}, bf16[1744,128]{1,0:T(8,128)(2,1)S(1)}, u32[]{:S(2)}, u32[]{:S(2)}) collective-permute-start(bf16[1744,128]{1,0:T(8,128)(2,1)S(1)} %slice.26), channel_id=1, source_target_pairs={{0,1},{1,2},{2,3},{3,4},{4,5},{5,6},{6,7},{7,8},{8,9},{9,10},{10,1... | collective-permute-start | bytes 1339400 | tf_op jit(solution)/shard_map/ppermute | solution.py:333
  62.2 12.2 %collective-permute-done.2.refs_0_ = bf16[1744,128]{1,0:T(8,128)(2,1)S(1)} collective-permute-done((bf16[1744,128]{1,0:T(8,128)(2,1)S(1)}, bf16[1744,128]{1,0:T(8,128)(2,1)S(1)}, u32[]{:S(2)}, u32[]{:S(2)}) %collective-permute-start.2) | collective-permute-done | bytes 446496 | tf_op jit(solution)/shard_map/ppermute | solution.py:333
  74.4 0.0 collective-permute-done.5.refs_6_
  74.4 2.3 %shard_map.30 = (bf16[1344,128]{1,0:T(8,128)(2,1)S(1)}, bf16[1216,128]{1,0:T(8,128)(2,1)S(1)}) custom-call(bf16[1744,128]{1,0:T(8,128)(2,1)S(1)} %collective-permute-done.2.refs_0_, bf16[2256,128]{1,0:T(8,128)(2,1)S(1)} %collective-permute-done.1.refs_1_, bf16[2768,128]{1,0:T(8,128)(2,1)S(1)} %collective-permute-done.refs_2_, ...), custom_call_target="tpu_custom_call" | custom-call | flops 1543503872 | bytes 6291456 | tf_op jit(solution)/shard_map/pallas_call | solution.py:269
  76.8 1.9 %collective-permute-start.6 = (bf16[1344,128]{1,0:T(8,128)(2,1)S(1)}, bf16[1344,128]{1,0:T(8,128)(2,1)S(1)}, u32[]{:S(2)}, u32[]{:S(2)}) collective-permute-start(bf16[1344,128]{1,0:T(8,128)(2,1)S(1)} %get-tuple-element.7), channel_id=1, source_target_pairs={{0,3},{1,4},{2,5},{3,6},{4,7},{5,8},{6,9},{7,10},{8,11},{9,12},{10... | collective-permute-start | bytes 1032200 | tf_op jit(solution)/shard_map/ppermute | solution.py:347
  78.7 8.8 %collective-permute-start.7 = (bf16[1216,128]{1,0:T(8,128)(2,1)S(1)}, bf16[1216,128]{1,0:T(8,128)(2,1)S(1)}, u32[]{:S(2)}, u32[]{:S(2)}) collective-permute-start(bf16[1216,128]{1,0:T(8,128)(2,1)S(1)} %get-tuple-element.8), channel_id=1, source_target_pairs={{0,509},{1,510},{2,511},{3,0},{4,1},{5,2},{6,3},{7,4},{8,5},{9,6},... | collective-permute-start | bytes 933896 | tf_op jit(solution)/shard_map/ppermute | solution.py:348
  87.5 7.7 %shard_map.29.part_ref = f32[256,1792]{1,0:T(8,128)S(1)} custom-call(bf16[1744,128]{1,0:T(8,128)(2,1)S(1)} %collective-permute-done.2.refs_0_, bf16[2256,128]{1,0:T(8,128)(2,1)S(1)} %collective-permute-done.1.refs_1_, bf16[2768,128]{1,0:T(8,128)(2,1)S(1)} %collective-permute-done.refs_2_, bf16[3104,128]{1,0:T(8,128)(2,1)S(1)} %shard_map.28.refs_3_.note_ref, ...), custom_call_target="tpu_custom_call" | custom-call | flops 7113539584 | bytes 6291456 | tf_op jit(solution)/shard_map/pallas_call | solution.py:269
  95.1 7.1 %collective-permute-done.7.down_ref = bf16[1216,128]{1,0:T(8,128)(2,1)S(1)} collective-permute-done((bf16[1216,128]{1,0:T(8,128)(2,1)S(1)}, bf16[1216,128]{1,0:T(8,128)(2,1)S(1)}, u32[]{:S(2)}, u32[]{:S(2)}) %collective-permute-start.7) | collective-permute-done | bytes 311328 | tf_op jit(solution)/shard_map/ppermute | solution.py:348
  102.2 0.0 collective-permute-done.6.up_ref
  102.2 1.4 %shard_map.31 = bf16[4,64,1536]{2,1,0:T(8,128)(2,1)} custom-call(f32[256,1792]{1,0:T(8,128)S(1)} %shard_map.29.part_ref, bf16[1344,128]{1,0:T(8,128)(2,1)S(1)} %collective-permute-done.6.up_ref, bf16[1216,128]{1,0:T(8,128)(2,1)S(1)} %collective-permute-done.7.down_ref, bf16[3104,128]{1,0:T(8,128)(2,1)S(1)} %shard_map.28.refs_3_.note_ref), custom_call_target="tpu_custom_call" | custom-call | flops 4194304 | bytes 4194304 | tf_op jit(solution)/shard_map/pallas_call | solution.py:312
  (6 shorter events, 0.2 us)
Async XLA Ops:
  0.0 1.1 %copy-start = (bf16[4,64,1536]{2,1,0:T(8,128)(2,1)S(1)}, bf16[4,64,1536]{2,1,0:T(8,128)(2,1)}, u32[]{:S(2)}) copy-start(bf16[4,64,1536]{2,1,0:T(8,128)(2,1)} %x_ref.1) | copy-start | bytes 2359300
  1.1 0.7 copy-start.1
  2.8 30.6 %collective-permute-start.3 = (bf16[2896,128]{1,0:T(8,128)(2,1)S(1)}, bf16[2896,128]{1,0:T(8,128)(2,1)S(1)}, u32[]{:S(2)}, u32[]{:S(2)}) collective-permute-start(bf16[2896,128]{1,0:T(8,128)(2,1)S(1)} %slice.27), channel_id=1, source_target_pairs={{0,511},{1,0},{2,1},{3,2},{4,3},{5,4},{6,5},{7,6},{8,7},{9,8},{10,... | collective-permute-start | bytes 2224136 | tf_op jit(solution)/shard_map/ppermute | solution.py:334
  17.1 24.1 %collective-permute-start = (bf16[2768,128]{1,0:T(8,128)(2,1)S(1)}, bf16[2768,128]{1,0:T(8,128)(2,1)S(1)}, u32[]{:S(2)}, u32[]{:S(2)}) collective-permute-start(bf16[2768,128]{1,0:T(8,128)(2,1)S(1)} %slice.24), channel_id=1, source_target_pairs={{0,1},{1,2},{2,3},{3,4},{4,5},{5,6},{6,7},{7,8},{8,9},{9,10},{10,1... | collective-permute-start | bytes 2125832 | tf_op jit(solution)/shard_map/ppermute | solution.py:333
  33.5 15.5 %collective-permute-start.4 = (bf16[2384,128]{1,0:T(8,128)(2,1)S(1)}, bf16[2384,128]{1,0:T(8,128)(2,1)S(1)}, u32[]{:S(2)}, u32[]{:S(2)}) collective-permute-start(bf16[2384,128]{1,0:T(8,128)(2,1)S(1)} %slice.28), channel_id=1, source_target_pairs={{0,511},{1,0},{2,1},{3,2},{4,3},{5,4},{6,5},{7,6},{8,7},{9,8},{10,... | collective-permute-start | bytes 1830920 | tf_op jit(solution)/shard_map/ppermute | solution.py:334
  41.2 19.0 %collective-permute-start.1 = (bf16[2256,128]{1,0:T(8,128)(2,1)S(1)}, bf16[2256,128]{1,0:T(8,128)(2,1)S(1)}, u32[]{:S(2)}, u32[]{:S(2)}) collective-permute-start(bf16[2256,128]{1,0:T(8,128)(2,1)S(1)} %slice.25), channel_id=1, source_target_pairs={{0,1},{1,2},{2,3},{3,4},{4,5},{5,6},{6,7},{7,8},{8,9},{9,10},{10,1... | collective-permute-start | bytes 1732616 | tf_op jit(solution)/shard_map/ppermute | solution.py:333
  49.0 25.4 %collective-permute-start.5 = (bf16[1872,128]{1,0:T(8,128)(2,1)S(1)}, bf16[1872,128]{1,0:T(8,128)(2,1)S(1)}, u32[]{:S(2)}, u32[]{:S(2)}) collective-permute-start(bf16[1872,128]{1,0:T(8,128)(2,1)S(1)} %slice.29), channel_id=1, source_target_pairs={{0,511},{1,0},{2,1},{3,2},{4,3},{5,4},{6,5},{7,6},{8,7},{9,8},{10,... | collective-permute-start | bytes 1437704 | tf_op jit(solution)/shard_map/ppermute | solution.py:334
  60.3 14.1 %collective-permute-start.2 = (bf16[1744,128]{1,0:T(8,128)(2,1)S(1)}, bf16[1744,128]{1,0:T(8,128)(2,1)S(1)}, u32[]{:S(2)}, u32[]{:S(2)}) collective-permute-start(bf16[1744,128]{1,0:T(8,128)(2,1)S(1)} %slice.26), channel_id=1, source_target_pairs={{0,1},{1,2},{2,3},{3,4},{4,5},{5,6},{6,7},{7,8},{8,9},{9,10},{10,1... | collective-permute-start | bytes 1339400 | tf_op jit(solution)/shard_map/ppermute | solution.py:333
  76.8 25.5 %collective-permute-start.6 = (bf16[1344,128]{1,0:T(8,128)(2,1)S(1)}, bf16[1344,128]{1,0:T(8,128)(2,1)S(1)}, u32[]{:S(2)}, u32[]{:S(2)}) collective-permute-start(bf16[1344,128]{1,0:T(8,128)(2,1)S(1)} %get-tuple-element.7), channel_id=1, source_target_pairs={{0,3},{1,4},{2,5},{3,6},{4,7},{5,8},{6,9},{7,10},{8,11},{9,12},{10... | collective-permute-start | bytes 1032200 | tf_op jit(solution)/shard_map/ppermute | solution.py:347
  78.7 23.6 %collective-permute-start.7 = (bf16[1216,128]{1,0:T(8,128)(2,1)S(1)}, bf16[1216,128]{1,0:T(8,128)(2,1)S(1)}, u32[]{:S(2)}, u32[]{:S(2)}) collective-permute-start(bf16[1216,128]{1,0:T(8,128)(2,1)S(1)} %get-tuple-element.8), channel_id=1, source_target_pairs={{0,509},{1,510},{2,511},{3,0},{4,1},{5,2},{6,3},{7,4},{8,5},{9,6},... | collective-permute-start | bytes 933896 | tf_op jit(solution)/shard_map/ppermute | solution.py:348

commit v3 on v2

--- a/solution.py
+++ b/solution.py
@@ -31,6 +31,9 @@
 
 def last_rows(tiles):
     return TAIL + (tiles - 1) * 2 * TILE
+
+
+SUMS = last_rows(REACH)
 
 
 def half_lanes(rows):
@@ -99,7 +102,7 @@
         out_shape=jax.ShapeDtypeStruct((ALL, 128), BF16),
         in_specs=[VMEM, SMEM],
         out_specs=VMEM,
-        compiler_params=pltpu.CompilerParams(vmem_limit_bytes=32 << 20),
+        compiler_params=pltpu.CompilerParams(vmem_limit_bytes=16 << 20),
         cost_estimate=pl.CostEstimate(flops=1 << 20, bytes_accessed=3 << 20, transcendentals=0),
     )(x, pattern)
 
@@ -227,31 +230,78 @@
         put(1, piece(3, 0))
         put(2, jnp.where(low, piece(1, 0), swap_halves(piece(3, 1))))
     else:
-        for half in range(2):
+        for q in range(ROWS):
+            put(q, piece(q, 0))
+        if tile == REACH - 1:
+            for q in range(2):
+                put(ROWS + q, jnp.where(low, piece(q, 1), swap_halves(piece(q + 2, 1))))
+        else:
             for q in range(ROWS):
-                put(half * ROWS + q, piece(q, half))
+                put(ROWS + q, piece(q, 1))
 
 
 def tile_rows(k):
     return slice((k + REACH) * TILE, (k + REACH + 1) * TILE)
 
 
-def edge_kernel(*refs):
-    up_ref, down_ref, window, square = refs[TILES:]
-    outer = {(REACH, k) for k in range(REACH)} | {(-REACH, -k) for k in range(REACH)}
-    load_window(refs, needed(UP_JOBS) | needed(DOWN_JOBS) | outer, window)
+def early_kernel(*refs):
+    up_ref, down_ref, near_ref, window, square = refs[TILES - 2 :]
+    refs = (None,) + refs[: TILES - 2] + (None,)
+    jobs = [[job for job in side if job[:2] != (0, 0)] for side in (UP_JOBS, DOWN_JOBS)]
+    rest = [(0, 0, 1 - REACH, -1), (0, 0, 1, REACH - 1)]
+    load_window(refs, needed(jobs[0] + jobs[1] + rest), window)
     notes = load_notes(refs, range(1 - REACH, REACH))
-    for jobs, row, cols, shift, first, out_ref in (
-        (UP_JOBS, REACH, range(REACH), 0, 0, up_ref),
-        (DOWN_JOBS, -REACH, range(1 - REACH, 1), 2 * REACH, REACH + 1, down_ref),
+    for side, out_ref in enumerate((up_ref, down_ref)):
+        square_tiles(jobs[side], window, notes, square)
+        _, _, first, last = rest[side]
+        depth = slice((first + REACH) * TILE, (last + REACH + 1) * TILE)
+        near_ref[side] = jnp.dot(window[tile_rows(0), depth], window[depth, tile_rows(0)], preferred_element_type=F32)
+        for k, c, _, _ in jobs[side]:
+            out_ref[abs(k) * TILE : abs(k) * TILE + TILE, abs(c) * TILE : abs(c) * TILE + TILE] = square[
+                tile_rows(k), tile_rows(c)
+            ]
+
+
+def edge_kernel(below_ref, own_ref, above_ref, up_square, down_square, near_ref, up_ref, down_ref, left, right):
+    note = spread(own_ref[:NOTE, :])[:, REACH * TILE : (REACH + 1) * TILE]
+    below_start = NOTE + tile_start(TILES - 1, 0)
+    for side, (k, far_ref, first, base, square, out_ref) in enumerate(
+        (
+            (REACH, above_ref, 0, NOTE, up_square, up_ref),
+            (-REACH, below_ref, REACH, 0, down_square, down_ref),
+        )
     ):
-        square_tiles(jobs, window, notes, square)
-        depth = slice((cols[0] + REACH) * TILE, (cols[-1] + REACH + 1) * TILE)
-        for c in cols:
+        for c in range(REACH):
+            j = (c if k > 0 else -c) - k + REACH
+            unpack_tile(far_ref, j, base + tile_start(j, first), left, 0, c * TILE)
+        if k > 0:
+            unpack_tile(own_ref, 0, NOTE, left, 0, REACH * TILE)
+            unpack_tile(below_ref, TILES - 1, tile_start(TILES - 1, REACH), right, 0, 0)
+        else:
+            unpack_tile(own_ref, TILES - 1, below_start, left, 0, REACH * TILE)
+            unpack_tile(above_ref, 0, NOTE, right, 0, 0)
+        near = near_ref[side] + jnp.dot(
+            left[:, REACH * TILE :], right[...], preferred_element_type=F32
+        )
+        near = jnp.concatenate(
+            [
+                jnp.where(note[q : q + 1] > 0.5, near[q * BLOCK : (q + 1) * BLOCK], 0.0).astype(BF16)
+                for q in range(ROWS)
+            ],
+            axis=0,
+        )
+        for c in range(REACH):
             total = jnp.dot(
-                window[tile_rows(row), depth], square[depth, tile_rows(c)], preferred_element_type=F32
+                left[:, TILE : REACH * TILE],
+                square[TILE:, c * TILE : (c + 1) * TILE],
+                preferred_element_type=F32,
             )
-            pack_tile(total, c + shift, first, out_ref)
+            first_row = near if c == 0 else square[:TILE, c * TILE : (c + 1) * TILE]
+            total = total + jnp.dot(left[:, :TILE], first_row, preferred_element_type=F32)
+            if k > 0:
+                pack_tile(total, c, 0, out_ref)
+            else:
+                pack_tile(total, 2 * REACH - c, REACH + 1, out_ref)
 
 
 def own_kernel(*refs):
@@ -265,26 +315,33 @@
         out_ref[:, tile_rows(c)] = 1.5 * x - 0.5 * total
 
 
-def window_call(kernel, products, out_shape, messages):
+def call(kernel, products, out_shape, scratch, limit, operands):
     return pl.pallas_call(
         kernel,
         out_shape=out_shape,
-        in_specs=[VMEM] * TILES,
+        in_specs=[VMEM] * len(operands),
         out_specs=jax.tree.map(lambda _: VMEM, out_shape),
-        scratch_shapes=[
-            pltpu.VMEM((TILES * TILE, TILES * TILE), BF16),
-            pltpu.VMEM((TILES * TILE, TILES * TILE), BF16),
-        ],
-        compiler_params=pltpu.CompilerParams(vmem_limit_bytes=48 << 20),
+        scratch_shapes=[pltpu.VMEM(shape, BF16) for shape in scratch],
+        compiler_params=pltpu.CompilerParams(vmem_limit_bytes=limit << 20),
         cost_estimate=pl.CostEstimate(
             flops=products * 2 * TILE**3, bytes_accessed=6 << 20, transcendentals=0
         ),
-    )(*messages)
+    )(*operands)
 
 
 def finish_kernel(part_ref, up_ref, down_ref, note_ref, out_ref, extra):
+    low = half_lanes(BLOCK)
     for tile in range(REACH):
-        unpack_tile(up_ref, tile, tile_start(tile, 0), extra, 0, tile * TILE)
+        if tile < REACH - 1:
+            unpack_tile(up_ref, tile, tile_start(tile, 0), extra, 0, tile * TILE)
+        else:
+            start = tile_start(tile, 0)
+            cols = slice(tile * TILE + 128, tile * TILE + 256)
+            extra[:, tile * TILE : tile * TILE + 128] = up_ref[start : start + TILE, :]
+            for q in range(2):
+                mixed = up_ref[start + TILE + q * BLOCK : start + TILE + (q + 1) * BLOCK, :]
+                extra[q * BLOCK : (q + 1) * BLOCK, cols] = jnp.where(low, mixed.astype(F32), 0.0).astype(BF16)
+                extra[(q + 2) * BLOCK : (q + 3) * BLOCK, cols] = jnp.where(low, swap_halves(mixed), 0.0).astype(BF16)
         far = REACH + 1 + tile
         unpack_tile(down_ref, far, tile_start(far, REACH + 1), extra, 0, (REACH + tile) * TILE)
     keep = spread(note_ref[:NOTE, :])
@@ -315,7 +372,7 @@
         in_specs=[VMEM] * 4,
         out_specs=VMEM,
         scratch_shapes=[pltpu.VMEM((TILE, 2 * REACH * TILE), BF16)],
-        compiler_params=pltpu.CompilerParams(vmem_limit_bytes=32 << 20),
+        compiler_params=pltpu.CompilerParams(vmem_limit_bytes=16 << 20),
         cost_estimate=pl.CostEstimate(flops=4 << 20, bytes_accessed=4 << 20, transcendentals=0),
     )(part, up, down, own)
 
@@ -333,17 +390,34 @@
         below = lax.ppermute(below[below.shape[0] - NOTE - last_rows(tiles) :], AXES, shift(1))
         above = lax.ppermute(above[: NOTE + first_rows(tiles)], AXES, shift(-1))
         held[-step], held[step] = below, above
-    messages = [held[k] for k in SPAN]
-    up, down = window_call(
+    wide = TILES * TILE
+    corner = jax.ShapeDtypeStruct((REACH * TILE, REACH * TILE), BF16)
+    sums = jax.ShapeDtypeStruct((SUMS, 128), BF16)
+    near = jax.ShapeDtypeStruct((2, TILE, TILE), F32)
+    early = call(
+        early_kernel,
+        28,
+        (corner, corner, near),
+        [(wide, wide), (wide, wide)],
+        24,
+        [held[k] for k in range(1 - REACH, REACH)],
+    )
+    up, down = call(
         edge_kernel,
-        46,
-        (
-            jax.ShapeDtypeStruct((first_rows(REACH), 128), BF16),
-            jax.ShapeDtypeStruct((last_rows(REACH), 128), BF16),
-        ),
-        messages,
+        20,
+        (sums, sums),
+        [(TILE, (REACH + 1) * TILE), (TILE, TILE)],
+        16,
+        [held[-REACH], own, held[REACH], *early],
     )
-    part = window_call(own_kernel, 212, jax.ShapeDtypeStruct((TILE, TILES * TILE), F32), messages)
+    part = call(
+        own_kernel,
+        212,
+        jax.ShapeDtypeStruct((TILE, wide), F32),
+        [(wide, wide), (wide, wide)],
+        32,
+        [held[k] for k in SPAN],
+    )
     up = lax.ppermute(up, AXES, shift(REACH))
     down = lax.ppermute(down, AXES, shift(-REACH))
     return finish(part, up, down, own, jax.ShapeDtypeStruct(x.shape, x.dtype))

time: 104 us -> 103 us (level)
  waiting for transfers between devices: 43.1 us -> 41.8 us
    ppermute x3, waiting for transfers between devices: 15.7 us -> 14.5 us  [per_device(): lax.ppermute(below[below.shape[0] - NOTE - last_rows(tiles):], AXES, shif...]
    pallas_call x2 -> x3, Pallas kernels: 10 us -> 9.97 us  [call(): pl.pallas_call(kernel, out_shape=out_shape, in_specs=[VMEM] * len(operand...]
  transfers between devices with their start and end apart: 8 -> 8, of which waited for: 5 -> 6; matrix products, arithmetic and copies ran while one was open for 0% -> 0% of each run, Pallas kernels for 7% -> 9%
where the time goes in v3:
time: 103 us; the launch traced here: 102 us
  starting transfers between devices  46.1 us (45%)
  waiting for transfers between devices  41.8 us (41%)
  Pallas kernels  12.3 us (12%)
  local copies, waits for them, and re-layouts  2.05 us (2%)
    ppermute x3, starting transfers between devices, per_device(): above = lax.ppermute(above[:NOTE + first_rows(tiles)], AXES, shift(-1))  29.7 us
    ppermute x3, waiting for transfers between devices, per_device(): above = lax.ppermute(above[:NOTE + first_rows(tiles)], AXES, shift(-1))  20.2 us
    ppermute x3, waiting for transfers between devices, per_device(): lax.ppermute(below[below.shape[0] - NOTE - last_rows(tiles):], AXES, shif...  14.5 us
    pallas_call x3, Pallas kernels, call(): pl.pallas_call(kernel, out_shape=out_shape, in_specs=[VMEM] * len(operand...  9.97 us
    ppermute x1, starting transfers between devices, per_device(): down = lax.ppermute(down, AXES, shift(-REACH))  8.76 us
    ppermute x1, waiting for transfers between devices, per_device(): down = lax.ppermute(down, AXES, shift(-REACH))  6.43 us
    ppermute x3, starting transfers between devices, per_device(): lax.ppermute(below[below.shape[0] - NOTE - last_rows(tiles):], AXES, shif...  5.76 us
  transfers between devices with their start and end apart: 8, of which 6 were waited for; matrix products, arithmetic and copies ran while one was open for 0% of the time, Pallas kernels for 9%

profile of v3, /device:TPU:1, one launch (start us, length us, event | category | flops | bytes accessed | tf_op | source)
XLA Modules:
  0.0 102.4 jit_solution(5909014147351337427)
XLA Ops:
  0.0 0.0 copy-start
  0.0 1.1 %copy-done = bf16[4,64,1536]{2,1,0:T(8,128)(2,1)S(1)} copy-done((bf16[4,64,1536]{2,1,0:T(8,128)(2,1)S(1)}, bf16[4,64,1536]{2,1,0:T(8,128)(2,1)}, u32[]{:S(2)}) %copy-start) | copy-done | bytes 786456
  1.1 0.7 copy-done.1
  1.8 0.9 shard_map.28.refs_3_.refs_2_.own_ref.note_ref
  2.8 14.3 %collective-permute-start.3 = (bf16[2896,128]{1,0:T(8,128)(2,1)S(1)}, bf16[2896,128]{1,0:T(8,128)(2,1)S(1)}, u32[]{:S(2)}, u32[]{:S(2)}) collective-permute-start(bf16[2896,128]{1,0:T(8,128)(2,1)S(1)} %slice.27), channel_id=1, source_target_pairs={{0,511},{1,0},{2,1},{3,2},{4,3},{5,4},{6,5},{7,6},{8,7},{9,8},{10,... | collective-permute-start | bytes 2224136 | tf_op jit(solution)/shard_map/ppermute | solution.py:391
  17.1 1.9 %collective-permute-start = (bf16[2768,128]{1,0:T(8,128)(2,1)S(1)}, bf16[2768,128]{1,0:T(8,128)(2,1)S(1)}, u32[]{:S(2)}, u32[]{:S(2)}) collective-permute-start(bf16[2768,128]{1,0:T(8,128)(2,1)S(1)} %slice.24), channel_id=1, source_target_pairs={{0,1},{1,2},{2,3},{3,4},{4,5},{5,6},{6,7},{7,8},{8,9},{9,10},{10,1... | collective-permute-start | bytes 2125832 | tf_op jit(solution)/shard_map/ppermute | solution.py:390
  19.0 14.4 %collective-permute-done.3.refs_4_.refs_3_ = bf16[2896,128]{1,0:T(8,128)(2,1)S(1)} collective-permute-done((bf16[2896,128]{1,0:T(8,128)(2,1)S(1)}, bf16[2896,128]{1,0:T(8,128)(2,1)S(1)}, u32[]{:S(2)}, u32[]{:S(2)}) %collective-permute-start.3) | collective-permute-done | bytes 741408 | tf_op jit(solution)/shard_map/ppermute | solution.py:391
  33.5 7.7 %collective-permute-start.4 = (bf16[2384,128]{1,0:T(8,128)(2,1)S(1)}, bf16[2384,128]{1,0:T(8,128)(2,1)S(1)}, u32[]{:S(2)}, u32[]{:S(2)}) collective-permute-start(bf16[2384,128]{1,0:T(8,128)(2,1)S(1)} %slice.28), channel_id=1, source_target_pairs={{0,511},{1,0},{2,1},{3,2},{4,3},{5,4},{6,5},{7,6},{8,7},{9,8},{10,... | collective-permute-start | bytes 1830920 | tf_op jit(solution)/shard_map/ppermute | solution.py:391
  41.2 0.0 collective-permute-done.refs_2_.refs_1_
  41.2 1.9 %collective-permute-start.1 = (bf16[2256,128]{1,0:T(8,128)(2,1)S(1)}, bf16[2256,128]{1,0:T(8,128)(2,1)S(1)}, u32[]{:S(2)}, u32[]{:S(2)}) collective-permute-start(bf16[2256,128]{1,0:T(8,128)(2,1)S(1)} %slice.25), channel_id=1, source_target_pairs={{0,1},{1,2},{2,3},{3,4},{4,5},{5,6},{6,7},{7,8},{8,9},{9,10},{10,1... | collective-permute-start | bytes 1732616 | tf_op jit(solution)/shard_map/ppermute | solution.py:390
  43.2 5.8 %collective-permute-done.4.refs_5_.refs_4_ = bf16[2384,128]{1,0:T(8,128)(2,1)S(1)} collective-permute-done((bf16[2384,128]{1,0:T(8,128)(2,1)S(1)}, bf16[2384,128]{1,0:T(8,128)(2,1)S(1)}, u32[]{:S(2)}, u32[]{:S(2)}) %collective-permute-start.4) | collective-permute-done | bytes 610336 | tf_op jit(solution)/shard_map/ppermute | solution.py:391
  49.0 7.7 %collective-permute-start.5 = (bf16[1872,128]{1,0:T(8,128)(2,1)S(1)}, bf16[1872,128]{1,0:T(8,128)(2,1)S(1)}, u32[]{:S(2)}, u32[]{:S(2)}) collective-permute-start(bf16[1872,128]{1,0:T(8,128)(2,1)S(1)} %slice.29), channel_id=1, source_target_pairs={{0,511},{1,0},{2,1},{3,2},{4,3},{5,4},{6,5},{7,6},{8,7},{9,8},{10,... | collective-permute-start | bytes 1437704 | tf_op jit(solution)/shard_map/ppermute | solution.py:391
  56.7 3.5 %collective-permute-done.1.refs_1_.refs_0_ = bf16[2256,128]{1,0:T(8,128)(2,1)S(1)} collective-permute-done((bf16[2256,128]{1,0:T(8,128)(2,1)S(1)}, bf16[2256,128]{1,0:T(8,128)(2,1)S(1)}, u32[]{:S(2)}, u32[]{:S(2)}) %collective-permute-start.1) | collective-permute-done | bytes 577568 | tf_op jit(solution)/shard_map/ppermute | solution.py:390
  60.3 1.9 %collective-permute-start.2 = (bf16[1744,128]{1,0:T(8,128)(2,1)S(1)}, bf16[1744,128]{1,0:T(8,128)(2,1)S(1)}, u32[]{:S(2)}, u32[]{:S(2)}) collective-permute-start(bf16[1744,128]{1,0:T(8,128)(2,1)S(1)} %slice.26), channel_id=1, source_target_pairs={{0,1},{1,2},{2,3},{3,4},{4,5},{5,6},{6,7},{7,8},{8,9},{9,10},{10,1... | collective-permute-start | bytes 1339400 | tf_op jit(solution)/shard_map/ppermute | solution.py:390
  62.2 1.2 %shard_map.30 = (bf16[768,768]{1,0:T(8,128)(2,1)S(1)}, bf16[768,768]{1,0:T(8,128)(2,1)S(1)}, f32[2,256,256]{2,1,0:T(8,128)S(1)}) custom-call(bf16[2256,128]{1,0:T(8,128)(2,1)S(1)} %collective-permute-done.1.refs_1_.refs_0_, bf16[2768,128]{1,0:T(8,128)(2,1)S(1)} %collective-permute-done.refs_2_.refs_1_, ...), custom_call_target="tpu_custom_call" | custom-call | flops 939524096 | bytes 6291456 | tf_op jit(solution)/shard_map/pallas_call | solution.py:319
  63.4 11.0 %collective-permute-done.2.refs_0_.below_ref = bf16[1744,128]{1,0:T(8,128)(2,1)S(1)} collective-permute-done((bf16[1744,128]{1,0:T(8,128)(2,1)S(1)}, bf16[1744,128]{1,0:T(8,128)(2,1)S(1)}, u32[]{:S(2)}, u32[]{:S(2)}) %collective-permute-start.2) | collective-permute-done | bytes 446496 | tf_op jit(solution)/shard_map/ppermute | solution.py:390
  74.4 0.0 collective-permute-done.5.refs_6_.above_ref
  74.4 1.1 %shard_map.31 = (bf16[1216,128]{1,0:T(8,128)(2,1)S(1)}, bf16[1216,128]{1,0:T(8,128)(2,1)S(1)}) custom-call(bf16[1744,128]{1,0:T(8,128)(2,1)S(1)} %collective-permute-done.2.refs_0_.below_ref, bf16[3104,128]{1,0:T(8,128)(2,1)S(1)} %shard_map.28.refs_3_.refs_2_.own_ref.note_ref, bf16[1872,128]{1,0:T(8,128)(2,1)S(1)} %collective-permute-done.5.refs_6_.above_ref, ...), custom_call_target="tpu_custom_call" | custom-call | flops 671088640 | bytes 6291456 | tf_op jit(solution)/shard_map/pallas_call | solution.py:319
  75.5 1.9 %collective-permute-start.6 = (bf16[1216,128]{1,0:T(8,128)(2,1)S(1)}, bf16[1216,128]{1,0:T(8,128)(2,1)S(1)}, u32[]{:S(2)}, u32[]{:S(2)}) collective-permute-start(bf16[1216,128]{1,0:T(8,128)(2,1)S(1)} %get-tuple-element.13), channel_id=1, source_target_pairs={{0,3},{1,4},{2,5},{3,6},{4,7},{5,8},{6,9},{7,10},{8,11},{9,12},{10... | collective-permute-start | bytes 933896 | tf_op jit(solution)/shard_map/ppermute | solution.py:421
  77.5 8.8 %collective-permute-start.7 = (bf16[1216,128]{1,0:T(8,128)(2,1)S(1)}, bf16[1216,128]{1,0:T(8,128)(2,1)S(1)}, u32[]{:S(2)}, u32[]{:S(2)}) collective-permute-start(bf16[1216,128]{1,0:T(8,128)(2,1)S(1)} %get-tuple-element.14), channel_id=1, source_target_pairs={{0,509},{1,510},{2,511},{3,0},{4,1},{5,2},{6,3},{7,4},{8,5},{9,6},... | collective-permute-start | bytes 933896 | tf_op jit(solution)/shard_map/ppermute | solution.py:422
  86.2 7.7 %shard_map.29.part_ref = f32[256,1792]{1,0:T(8,128)S(1)} custom-call(bf16[1744,128]{1,0:T(8,128)(2,1)S(1)} %collective-permute-done.2.refs_0_.below_ref, bf16[2256,128]{1,0:T(8,128)(2,1)S(1)} %collective-permute-done.1.refs_1_.refs_0_, bf16[2768,128]{1,0:T(8,128)(2,1)S(1)} %collective-permute-done.refs_2_.refs_1_, ...), custom_call_target="tpu_custom_call" | custom-call | flops 7113539584 | bytes 6291456 | tf_op jit(solution)/shard_map/pallas_call | solution.py:319
  93.9 0.7 collective-permute-done.6.up_ref
  94.6 6.4 %collective-permute-done.7.down_ref = bf16[1216,128]{1,0:T(8,128)(2,1)S(1)} collective-permute-done((bf16[1216,128]{1,0:T(8,128)(2,1)S(1)}, bf16[1216,128]{1,0:T(8,128)(2,1)S(1)}, u32[]{:S(2)}, u32[]{:S(2)}) %collective-permute-start.7) | collective-permute-done | bytes 311328 | tf_op jit(solution)/shard_map/ppermute | solution.py:422
  101.0 1.4 %shard_map.32 = bf16[4,64,1536]{2,1,0:T(8,128)(2,1)} custom-call(f32[256,1792]{1,0:T(8,128)S(1)} %shard_map.29.part_ref, bf16[1216,128]{1,0:T(8,128)(2,1)S(1)} %collective-permute-done.6.up_ref, bf16[1216,128]{1,0:T(8,128)(2,1)S(1)} %collective-permute-done.7.down_ref, bf16[3104,128]{1,0:T(8,128)(2,1)S(1)} %shard_map.28.refs_3_.refs_2_.own_ref.note_ref), custom_call_target="tpu_custom_call" | custom-call | flops 4194304 | bytes 4194304 | tf_op jit(solution)/shard_map/pallas_call | solution.py:369
  (7 shorter events, 0.2 us)
Async XLA Ops:
  0.0 1.1 %copy-start = (bf16[4,64,1536]{2,1,0:T(8,128)(2,1)S(1)}, bf16[4,64,1536]{2,1,0:T(8,128)(2,1)}, u32[]{:S(2)}) copy-start(bf16[4,64,1536]{2,1,0:T(8,128)(2,1)} %x_ref.1) | copy-start | bytes 2359300
  1.1 0.7 copy-start.1
  2.8 30.6 %collective-permute-start.3 = (bf16[2896,128]{1,0:T(8,128)(2,1)S(1)}, bf16[2896,128]{1,0:T(8,128)(2,1)S(1)}, u32[]{:S(2)}, u32[]{:S(2)}) collective-permute-start(bf16[2896,128]{1,0:T(8,128)(2,1)S(1)} %slice.27), channel_id=1, source_target_pairs={{0,511},{1,0},{2,1},{3,2},{4,3},{5,4},{6,5},{7,6},{8,7},{9,8},{10,... | collective-permute-start | bytes 2224136 | tf_op jit(solution)/shard_map/ppermute | solution.py:391
  17.1 24.1 %collective-permute-start = (bf16[2768,128]{1,0:T(8,128)(2,1)S(1)}, bf16[2768,128]{1,0:T(8,128)(2,1)S(1)}, u32[]{:S(2)}, u32[]{:S(2)}) collective-permute-start(bf16[2768,128]{1,0:T(8,128)(2,1)S(1)} %slice.24), channel_id=1, source_target_pairs={{0,1},{1,2},{2,3},{3,4},{4,5},{5,6},{6,7},{7,8},{8,9},{9,10},{10,1... | collective-permute-start | bytes 2125832 | tf_op jit(solution)/shard_map/ppermute | solution.py:390
  33.5 15.5 %collective-permute-start.4 = (bf16[2384,128]{1,0:T(8,128)(2,1)S(1)}, bf16[2384,128]{1,0:T(8,128)(2,1)S(1)}, u32[]{:S(2)}, u32[]{:S(2)}) collective-permute-start(bf16[2384,128]{1,0:T(8,128)(2,1)S(1)} %slice.28), channel_id=1, source_target_pairs={{0,511},{1,0},{2,1},{3,2},{4,3},{5,4},{6,5},{7,6},{8,7},{9,8},{10,... | collective-permute-start | bytes 1830920 | tf_op jit(solution)/shard_map/ppermute | solution.py:391
  41.2 19.0 %collective-permute-start.1 = (bf16[2256,128]{1,0:T(8,128)(2,1)S(1)}, bf16[2256,128]{1,0:T(8,128)(2,1)S(1)}, u32[]{:S(2)}, u32[]{:S(2)}) collective-permute-start(bf16[2256,128]{1,0:T(8,128)(2,1)S(1)} %slice.25), channel_id=1, source_target_pairs={{0,1},{1,2},{2,3},{3,4},{4,5},{5,6},{6,7},{7,8},{8,9},{9,10},{10,1... | collective-permute-start | bytes 1732616 | tf_op jit(solution)/shard_map/ppermute | solution.py:390
  49.0 25.4 %collective-permute-start.5 = (bf16[1872,128]{1,0:T(8,128)(2,1)S(1)}, bf16[1872,128]{1,0:T(8,128)(2,1)S(1)}, u32[]{:S(2)}, u32[]{:S(2)}) collective-permute-start(bf16[1872,128]{1,0:T(8,128)(2,1)S(1)} %slice.29), channel_id=1, source_target_pairs={{0,511},{1,0},{2,1},{3,2},{4,3},{5,4},{6,5},{7,6},{8,7},{9,8},{10,... | collective-permute-start | bytes 1437704 | tf_op jit(solution)/shard_map/ppermute | solution.py:391
  60.3 14.1 %collective-permute-start.2 = (bf16[1744,128]{1,0:T(8,128)(2,1)S(1)}, bf16[1744,128]{1,0:T(8,128)(2,1)S(1)}, u32[]{:S(2)}, u32[]{:S(2)}) collective-permute-start(bf16[1744,128]{1,0:T(8,128)(2,1)S(1)} %slice.26), channel_id=1, source_target_pairs={{0,1},{1,2},{2,3},{3,4},{4,5},{5,6},{6,7},{7,8},{8,9},{9,10},{10,1... | collective-permute-start | bytes 1339400 | tf_op jit(solution)/shard_map/ppermute | solution.py:390
  75.5 19.1 %collective-permute-start.6 = (bf16[1216,128]{1,0:T(8,128)(2,1)S(1)}, bf16[1216,128]{1,0:T(8,128)(2,1)S(1)}, u32[]{:S(2)}, u32[]{:S(2)}) collective-permute-start(bf16[1216,128]{1,0:T(8,128)(2,1)S(1)} %get-tuple-element.13), channel_id=1, source_target_pairs={{0,3},{1,4},{2,5},{3,6},{4,7},{5,8},{6,9},{7,10},{8,11},{9,12},{10... | collective-permute-start | bytes 933896 | tf_op jit(solution)/shard_map/ppermute | solution.py:421
  77.5 23.6 %collective-permute-start.7 = (bf16[1216,128]{1,0:T(8,128)(2,1)S(1)}, bf16[1216,128]{1,0:T(8,128)(2,1)S(1)}, u32[]{:S(2)}, u32[]{:S(2)}) collective-permute-start(bf16[1216,128]{1,0:T(8,128)(2,1)S(1)} %get-tuple-element.14), channel_id=1, source_target_pairs={{0,509},{1,510},{2,511},{3,0},{4,1},{5,2},{6,3},{7,4},{8,5},{9,6},... | collective-permute-start | bytes 933896 | tf_op jit(solution)/shard_map/ppermute | solution.py:422

commit v4 on v3

--- a/solution.py
+++ b/solution.py
@@ -19,6 +19,7 @@
 DATA = HEAD + BODY + TAIL
 NOTE = 16
 ALL = NOTE + DATA + NOTE
+PAD = HEAD - TAIL
 F32 = jnp.float32
 BF16 = jnp.bfloat16
 VMEM = pl.BlockSpec(memory_space=pltpu.VMEM)
@@ -44,7 +45,7 @@
     return pltpu.roll(piece.astype(F32), BLOCK, 1)
 
 
-def pack_kernel(x_ref, pattern_ref, out_ref):
+def pack_kernel(odd_ref, x_ref, pattern_ref, out_ref, sent_ref):
     low = half_lanes(BLOCK)
     zero = jnp.zeros((BLOCK, 128), F32)
     note = jnp.zeros((NOTE, 128), F32)
@@ -94,17 +95,24 @@
     )
     out_ref[:NOTE, :] = note.astype(BF16)
     out_ref[NOTE + DATA :, :] = note.astype(BF16)
-
-
-def pack(x, pattern):
+    rows = sent_ref.shape[1]
+    odd = odd_ref[0]
+    sent_ref[odd] = out_ref[:rows, :]
+    sent_ref[1 - odd] = out_ref[ALL - rows :, :]
+
+
+def pack(parity, x, pattern):
     return pl.pallas_call(
         pack_kernel,
-        out_shape=jax.ShapeDtypeStruct((ALL, 128), BF16),
-        in_specs=[VMEM, SMEM],
-        out_specs=VMEM,
+        out_shape=(
+            jax.ShapeDtypeStruct((ALL, 128), BF16),
+            jax.ShapeDtypeStruct((2, NOTE + first_rows(TILES - 1), 128), BF16),
+        ),
+        in_specs=[SMEM, VMEM, SMEM],
+        out_specs=(VMEM, VMEM),
         compiler_params=pltpu.CompilerParams(vmem_limit_bytes=16 << 20),
         cost_estimate=pl.CostEstimate(flops=1 << 20, bytes_accessed=3 << 20, transcendentals=0),
-    )(x, pattern)
+    )(parity, x, pattern)
 
 
 def unpack_tile(source, tile, base, window, row, col):
@@ -160,7 +168,7 @@
     return jnp.dot(note, jnp.where(lane == block, 1.0, 0.0).astype(BF16), preferred_element_type=F32)
 
 
-def square_tiles(jobs, window, notes, square):
+def square_tiles(jobs, window, notes, square, rest=None):
     for k, c, first, last in jobs:
         depth = slice((first + REACH) * TILE, (last + REACH + 1) * TILE)
         total = jnp.dot(
@@ -171,9 +179,12 @@
         place = (c - k + REACH) * TILE
         for q in range(ROWS):
             keep = notes[k][q : q + 1, place : place + TILE] > 0.5
-            square[
-                pl.ds((k + REACH) * TILE + q * BLOCK, BLOCK), pl.ds((c + REACH) * TILE, TILE)
-            ] = jnp.where(keep, total[q * BLOCK : (q + 1) * BLOCK], 0.0).astype(BF16)
+            value = jnp.where(keep, total[q * BLOCK : (q + 1) * BLOCK], 0.0)
+            rounded = value.astype(BF16)
+            at = pl.ds((k + REACH) * TILE + q * BLOCK, BLOCK), pl.ds((c + REACH) * TILE, TILE)
+            square[at] = rounded
+            if rest is not None and k * c > 0:
+                rest[at] = (value - rounded.astype(F32)).astype(BF16)
 
 
 SPAN = range(-REACH, REACH + 1)
@@ -192,7 +203,7 @@
     for r, t in sorted(tiles):
         j = t - r + REACH
         first = max(-r, 0)
-        base = 0 if r < 0 else NOTE
+        base = PAD if r < 0 else NOTE
         unpack_tile(
             refs[r + REACH],
             j,
@@ -268,7 +279,7 @@
     for side, (k, far_ref, first, base, square, out_ref) in enumerate(
         (
             (REACH, above_ref, 0, NOTE, up_square, up_ref),
-            (-REACH, below_ref, REACH, 0, down_square, down_ref),
+            (-REACH, below_ref, REACH, PAD, down_square, down_ref),
         )
     ):
         for c in range(REACH):
@@ -276,7 +287,7 @@
             unpack_tile(far_ref, j, base + tile_start(j, first), left, 0, c * TILE)
         if k > 0:
             unpack_tile(own_ref, 0, NOTE, left, 0, REACH * TILE)
-            unpack_tile(below_ref, TILES - 1, tile_start(TILES - 1, REACH), right, 0, 0)
+            unpack_tile(below_ref, TILES - 1, PAD + tile_start(TILES - 1, REACH), right, 0, 0)
         else:
             unpack_tile(own_ref, TILES - 1, below_start, left, 0, REACH * TILE)
             unpack_tile(above_ref, 0, NOTE, right, 0, 0)
@@ -305,12 +316,19 @@
 
 
 def own_kernel(*refs):
-    out_ref, window, square = refs[TILES:]
+    out_ref, keep_ref, window, square, rest = refs[TILES:]
     load_window(refs, needed(OWN_JOBS), window)
-    square_tiles(OWN_JOBS, window, load_notes(refs, SPAN), square)
+    notes = load_notes(refs, SPAN)
+    keep_ref[...] = notes[0]
+    square_tiles(OWN_JOBS, window, notes, square, rest)
     for c in SPAN:
         depth = slice(max(c, 0) * TILE, (min(c, 0) + TILES) * TILE)
         total = jnp.dot(window[tile_rows(0), depth], square[depth, tile_rows(c)], preferred_element_type=F32)
+        if c:
+            depth = slice(0, REACH * TILE) if c < 0 else slice((REACH + 1) * TILE, TILES * TILE)
+            total = total + jnp.dot(
+                window[tile_rows(0), depth], rest[depth, tile_rows(c)], preferred_element_type=F32
+            )
         x = window[tile_rows(0), tile_rows(c)].astype(F32)
         out_ref[:, tile_rows(c)] = 1.5 * x - 0.5 * total
 
@@ -329,7 +347,7 @@
     )(*operands)
 
 
-def finish_kernel(part_ref, up_ref, down_ref, note_ref, out_ref, extra):
+def finish_kernel(part_ref, up_ref, down_ref, keep_ref, out_ref, extra):
     low = half_lanes(BLOCK)
     for tile in range(REACH):
         if tile < REACH - 1:
@@ -344,7 +362,6 @@
                 extra[(q + 2) * BLOCK : (q + 3) * BLOCK, cols] = jnp.where(low, swap_halves(mixed), 0.0).astype(BF16)
         far = REACH + 1 + tile
         unpack_tile(down_ref, far, tile_start(far, REACH + 1), extra, 0, (REACH + tile) * TILE)
-    keep = spread(note_ref[:NOTE, :])
     width = out_ref.shape[2]
     side = REACH * TILE
     for q in range(ROWS):
@@ -358,14 +375,14 @@
             ],
             axis=1,
         )
-        strip = jnp.where(keep[q : q + 1] > 0.5, strip, 0.0)
+        strip = jnp.where(keep_ref[q : q + 1, :] > 0.5, strip, 0.0)
         if q % 2:
             strip = pltpu.roll(strip, TILES * TILE - BLOCK, 1)
         start = (q // 2) * 128
         out_ref[q] = strip[:, start : start + width].astype(BF16)
 
 
-def finish(part, up, down, own, out_type):
+def finish(part, up, down, keep, out_type):
     return pl.pallas_call(
         finish_kernel,
         out_shape=out_type,
@@ -374,21 +391,33 @@
         scratch_shapes=[pltpu.VMEM((TILE, 2 * REACH * TILE), BF16)],
         compiler_params=pltpu.CompilerParams(vmem_limit_bytes=16 << 20),
         cost_estimate=pl.CostEstimate(flops=4 << 20, bytes_accessed=4 << 20, transcendentals=0),
-    )(part, up, down, own)
+    )(part, up, down, keep)
 
 
 def per_device(count, x, pattern):
+    odd = lax.axis_index(AXES[1]) % 2
+    parity = jnp.reshape(odd, (1,)).astype(jnp.int32)
+    outer = [(n, (n + 1) % count if n % 2 else (n - 1) % count) for n in range(count)]
+    inner = [(n, n - 1 if n % 2 else n + 1) for n in range(count)]
+
     def shift(steps):
         return [(n, (n + steps) % count) for n in range(count)]
 
-    own = pack(x, pattern)
+    def cut(message, rows, upward):
+        return lax.dynamic_slice_in_dim(message, upward * (message.shape[0] - rows), rows, 0)
+
+    own, sent = pack(parity, x, pattern)
     held = {0: own}
-    below = own
-    above = own
-    for step in range(1, REACH + 1):
-        tiles = TILES - step
-        below = lax.ppermute(below[below.shape[0] - NOTE - last_rows(tiles) :], AXES, shift(1))
-        above = lax.ppermute(above[: NOTE + first_rows(tiles)], AXES, shift(-1))
+    from_outer = lax.ppermute(sent[0], AXES, outer)
+    from_inner = lax.ppermute(sent[1], AXES, inner)
+    below = held[-1] = jnp.where(odd == 1, from_inner, from_outer)
+    above = held[1] = jnp.where(odd == 1, from_outer, from_inner)
+    for step in range(2, REACH + 1):
+        rows = NOTE + first_rows(TILES - step)
+        below, above = (
+            lax.ppermute(below[below.shape[0] - rows :], AXES, shift(1)),
+            lax.ppermute(above[:rows], AXES, shift(-1)),
+        )
         held[-step], held[step] = below, above
     wide = TILES * TILE
     corner = jax.ShapeDtypeStruct((REACH * TILE, REACH * TILE), BF16)
@@ -410,17 +439,17 @@
         16,
         [held[-REACH], own, held[REACH], *early],
     )
-    part = call(
+    part, keep = call(
         own_kernel,
-        212,
-        jax.ShapeDtypeStruct((TILE, wide), F32),
-        [(wide, wide), (wide, wide)],
-        32,
+        230,
+        (jax.ShapeDtypeStruct((TILE, wide), F32), jax.ShapeDtypeStruct((NOTE, wide), F32)),
+        [(wide, wide), (wide, wide), (wide, wide)],
+        36,
         [held[k] for k in SPAN],
     )
     up = lax.ppermute(up, AXES, shift(REACH))
     down = lax.ppermute(down, AXES, shift(-REACH))
-    return finish(part, up, down, own, jax.ShapeDtypeStruct(x.shape, x.dtype))
+    return finish(part, up, down, keep, jax.ShapeDtypeStruct(x.shape, x.dtype))
 
 
 def solution(mesh):

time: 103 us -> 102 us (level)
  waiting for transfers between devices: 41.8 us -> 39.5 us
    ppermute x1, waiting for transfers between devices: 0.7 us -> 7.98 us  [per_device(): up = lax.ppermute(up, AXES, shift(REACH))]
    ppermute x6, waiting for transfers between devices: 34.7 us -> 29.9 us  [the longest x1 16.5 us: per_device(): from_outer = lax.ppermute(sent[0], AXES, outer)]
    ppermute x1, waiting for transfers between devices: 6.43 us -> 1.66 us  [per_device(): down = lax.ppermute(down, AXES, shift(-REACH))]
  transfers between devices with their start and end apart: 8 -> 8, of which waited for: 6 -> 7; matrix products, arithmetic and copies ran while one was open for 0% -> 0% of each run, Pallas kernels for 9% -> 9%
where the time goes in v4:
time: 102 us; the launch traced here: 101 us
  starting transfers between devices  45.1 us (44%)
  waiting for transfers between devices  39.5 us (39%)
  Pallas kernels  13.1 us (13%)
  local copies, waits for them, and re-layouts  2.92 us (3%)
    ppermute x1, waiting for transfers between devices, per_device(): from_outer = lax.ppermute(sent[0], AXES, outer)  16.5 us
    ppermute x2, starting transfers between devices, per_device(): lax.ppermute(above[:rows], AXES, shift(-1))  13.9 us
    ppermute x2, waiting for transfers between devices, per_device(): lax.ppermute(below[below.shape[0] - rows:], AXES, shift(1))  12.4 us
    ppermute x1, starting transfers between devices, per_device(): from_outer = lax.ppermute(sent[0], AXES, outer)  11.9 us
    pallas_call x3, Pallas kernels, call(): pl.pallas_call(kernel, out_shape=out_shape, in_specs=[VMEM] * len(operand...  10.7 us
    ppermute x1, starting transfers between devices, per_device(): down = lax.ppermute(down, AXES, shift(-REACH))  8.76 us
    ppermute x1, waiting for transfers between devices, per_device(): up = lax.ppermute(up, AXES, shift(REACH))  7.98 us
    ppermute x1, starting transfers between devices, per_device(): from_inner = lax.ppermute(sent[1], AXES, inner)  4.82 us
  transfers between devices with their start and end apart: 8, of which 7 were waited for; matrix products, arithmetic and copies ran while one was open for 0% of the time, Pallas kernels for 9%

profile of v4, /device:TPU:1, one launch (start us, length us, event | category | flops | bytes accessed | tf_op | source)
XLA Modules:
  0.0 100.9 jit_solution(15381207635387988696)
XLA Ops:
  0.0 1.1 %copy-done = bf16[4,64,1536]{2,1,0:T(8,128)(2,1)S(1)} copy-done((bf16[4,64,1536]{2,1,0:T(8,128)(2,1)S(1)}, bf16[4,64,1536]{2,1,0:T(8,128)(2,1)}, u32[]{:S(2)}) %copy-start) | copy-done | bytes 786456
  1.1 0.7 copy-done.1
  1.8 1.1 %shard_map.28 = (bf16[3104,128]{1,0:T(8,128)(2,1)S(1)}, bf16[2,2896,128]{2,1,0:T(8,128)(2,1)S(1)}) custom-call(s32[1]{0:T(128)} %bitcast.odd_ref, bf16[4,64,1536]{2,1,0:T(8,128)(2,1)S(1)} %copy-done, s32[4,24]{1,0:T(4,128)S(1)} %copy-done.1), custom_call_target="tpu_custom_call" | custom-call | flops 1048576 | bytes 3145728 | tf_op jit(solution)/shard_map/pallas_call | solution.py:105
  3.0 1.0 slice_bitcast_fusion
  3.9 4.8 %collective-permute-start = (bf16[2896,128]{1,0:T(8,128)(2,1)}, bf16[2896,128]{1,0:T(8,128)(2,1)S(1)}, u32[]{:S(2)}, u32[]{:S(2)}) collective-permute-start(bf16[2896,128]{1,0:T(8,128)(2,1)} %get-tuple-element.26), channel_id=1, source_target_pairs={{0,1},{1,0},{2,3},{3,2},{4,5},{5,4},{6,7},{7,6},{8,9},{9,8},{10,11... | collective-permute-start | bytes 2224136 | tf_op jit(solution)/shard_map/ppermute | solution.py:412
  8.7 11.9 %collective-permute-start.1 = (bf16[2896,128]{1,0:T(8,128)(2,1)S(1)}, bf16[2896,128]{1,0:T(8,128)(2,1)S(1)}, u32[]{:S(2)}, u32[]{:S(2)}) collective-permute-start(bf16[2896,128]{1,0:T(8,128)(2,1)S(1)} %get-tuple-element.25), channel_id=1, source_target_pairs={{0,511},{1,2},{2,1},{3,4},{4,3},{5,6},{6,5},{7,8},{8,7},{9,10},{10... | collective-permute-start | bytes 2224136 | tf_op jit(solution)/shard_map/ppermute | solution.py:411
  20.6 0.6 collective-permute-done
  21.2 16.5 %collective-permute-done.1 = bf16[2896,128]{1,0:T(8,128)(2,1)S(1)} collective-permute-done((bf16[2896,128]{1,0:T(8,128)(2,1)S(1)}, bf16[2896,128]{1,0:T(8,128)(2,1)S(1)}, u32[]{:S(2)}, u32[]{:S(2)}) %collective-permute-start.1) | collective-permute-done | bytes 741408 | tf_op jit(solution)/shard_map/ppermute | solution.py:411
  37.8 0.1 broadcast_select_fusion
  37.9 1.9 %collective-permute-start.2 = (bf16[2384,128]{1,0:T(8,128)(2,1)S(1)}, bf16[2384,128]{1,0:T(8,128)(2,1)S(1)}, u32[]{:S(2)}, u32[]{:S(2)}) collective-permute-start(bf16[2384,128]{1,0:T(8,128)(2,1)S(1)} %slice.24), channel_id=1, source_target_pairs={{0,1},{1,2},{2,3},{3,4},{4,5},{5,6},{6,7},{7,8},{8,9},{9,10},{10,1... | collective-permute-start | bytes 1830920 | tf_op jit(solution)/shard_map/ppermute | solution.py:418
  39.9 7.0 %collective-permute-start.4 = (bf16[2384,128]{1,0:T(8,128)(2,1)S(1)}, bf16[2384,128]{1,0:T(8,128)(2,1)S(1)}, u32[]{:S(2)}, u32[]{:S(2)}) collective-permute-start(bf16[2384,128]{1,0:T(8,128)(2,1)S(1)} %slice.26), channel_id=1, source_target_pairs={{0,511},{1,0},{2,1},{3,2},{4,3},{5,4},{6,5},{7,6},{8,7},{9,8},{10,... | collective-permute-start | bytes 1830920 | tf_op jit(solution)/shard_map/ppermute | solution.py:419
  46.9 8.4 %collective-permute-done.2.refs_1_.refs_0_ = bf16[2384,128]{1,0:T(8,128)(2,1)S(1)} collective-permute-done((bf16[2384,128]{1,0:T(8,128)(2,1)S(1)}, bf16[2384,128]{1,0:T(8,128)(2,1)S(1)}, u32[]{:S(2)}, u32[]{:S(2)}) %collective-permute-start.2) | collective-permute-done | bytes 610336 | tf_op jit(solution)/shard_map/ppermute | solution.py:418
  55.3 1.9 %collective-permute-start.3 = (bf16[1872,128]{1,0:T(8,128)(2,1)S(1)}, bf16[1872,128]{1,0:T(8,128)(2,1)S(1)}, u32[]{:S(2)}, u32[]{:S(2)}) collective-permute-start(bf16[1872,128]{1,0:T(8,128)(2,1)S(1)} %slice.25), channel_id=1, source_target_pairs={{0,1},{1,2},{2,3},{3,4},{4,5},{5,6},{6,7},{7,8},{8,9},{9,10},{10,1... | collective-permute-start | bytes 1437704 | tf_op jit(solution)/shard_map/ppermute | solution.py:418
  57.2 7.0 %collective-permute-start.5 = (bf16[1872,128]{1,0:T(8,128)(2,1)S(1)}, bf16[1872,128]{1,0:T(8,128)(2,1)S(1)}, u32[]{:S(2)}, u32[]{:S(2)}) collective-permute-start(bf16[1872,128]{1,0:T(8,128)(2,1)S(1)} %slice.27), channel_id=1, source_target_pairs={{0,511},{1,0},{2,1},{3,2},{4,3},{5,4},{6,5},{7,6},{8,7},{9,8},{10,... | collective-permute-start | bytes 1437704 | tf_op jit(solution)/shard_map/ppermute | solution.py:419
  64.2 1.2 %shard_map.30 = (bf16[768,768]{1,0:T(8,128)(2,1)S(1)}, bf16[768,768]{1,0:T(8,128)(2,1)S(1)}, f32[2,256,256]{2,1,0:T(8,128)S(1)}) custom-call(bf16[2384,128]{1,0:T(8,128)(2,1)S(1)} %collective-permute-done.2.refs_1_.refs_0_, bf16[2896,128]{1,0:T(8,128)(2,1)S(1)} %get-tuple-element.24.refs_2_.refs_1_, ...), custom_call_target="tpu_custom_call" | custom-call | flops 939524096 | bytes 6291456 | tf_op jit(solution)/shard_map/pallas_call | solution.py:337
  65.4 4.0 %collective-permute-done.3.refs_0_.below_ref = bf16[1872,128]{1,0:T(8,128)(2,1)S(1)} collective-permute-done((bf16[1872,128]{1,0:T(8,128)(2,1)S(1)}, bf16[1872,128]{1,0:T(8,128)(2,1)S(1)}, u32[]{:S(2)}, u32[]{:S(2)}) %collective-permute-start.3) | collective-permute-done | bytes 479264 | tf_op jit(solution)/shard_map/ppermute | solution.py:418
  69.4 0.4 collective-permute-done.5.refs_6_.above_ref
  69.8 1.1 %shard_map.31 = (bf16[1216,128]{1,0:T(8,128)(2,1)S(1)}, bf16[1216,128]{1,0:T(8,128)(2,1)S(1)}) custom-call(bf16[1872,128]{1,0:T(8,128)(2,1)S(1)} %collective-permute-done.3.refs_0_.below_ref, bf16[3104,128]{1,0:T(8,128)(2,1)S(1)} %get-tuple-element.15.refs_3_.refs_2_.own_ref, bf16[1872,128]{1,0:T(8,128)(2,1)S(1)} %collective-permute-done.5.refs_6_.above_ref, ...), custom_call_target="tpu_custom_call" | custom-call | flops 671088640 | bytes 6291456 | tf_op jit(solution)/shard_map/pallas_call | solution.py:337
  70.9 1.9 %collective-permute-start.6 = (bf16[1216,128]{1,0:T(8,128)(2,1)S(1)}, bf16[1216,128]{1,0:T(8,128)(2,1)S(1)}, u32[]{:S(2)}, u32[]{:S(2)}) collective-permute-start(bf16[1216,128]{1,0:T(8,128)(2,1)S(1)} %get-tuple-element.20), channel_id=1, source_target_pairs={{0,3},{1,4},{2,5},{3,6},{4,7},{5,8},{6,9},{7,10},{8,11},{9,12},{10... | collective-permute-start | bytes 933896 | tf_op jit(solution)/shard_map/ppermute | solution.py:450
  72.9 8.8 %collective-permute-start.7 = (bf16[1216,128]{1,0:T(8,128)(2,1)S(1)}, bf16[1216,128]{1,0:T(8,128)(2,1)S(1)}, u32[]{:S(2)}, u32[]{:S(2)}) collective-permute-start(bf16[1216,128]{1,0:T(8,128)(2,1)S(1)} %get-tuple-element.21), channel_id=1, source_target_pairs={{0,509},{1,510},{2,511},{3,0},{4,1},{5,2},{6,3},{7,4},{8,5},{9,6},... | collective-permute-start | bytes 933896 | tf_op jit(solution)/shard_map/ppermute | solution.py:451
  81.6 8.4 %shard_map.29 = (f32[256,1792]{1,0:T(8,128)S(1)}, f32[16,1792]{1,0:T(8,128)S(1)}) custom-call(bf16[1872,128]{1,0:T(8,128)(2,1)S(1)} %collective-permute-done.3.refs_0_.below_ref, bf16[2384,128]{1,0:T(8,128)(2,1)S(1)} %collective-permute-done.2.refs_1_.refs_0_, bf16[2896,128]{1,0:T(8,128)(2,1)S(1)} %get-tuple-element.24.refs_2_.refs_1_, ...), custom_call_target="tpu_custom_call" | custom-call | flops 7717519360 | bytes 6291456 | tf_op jit(solution)/shard_map/pallas_call | solution.py:337
  90.0 8.0 %collective-permute-done.6.up_ref = bf16[1216,128]{1,0:T(8,128)(2,1)S(1)} collective-permute-done((bf16[1216,128]{1,0:T(8,128)(2,1)S(1)}, bf16[1216,128]{1,0:T(8,128)(2,1)S(1)}, u32[]{:S(2)}, u32[]{:S(2)}) %collective-permute-start.6) | collective-permute-done | bytes 311328 | tf_op jit(solution)/shard_map/ppermute | solution.py:450
  98.0 1.7 %collective-permute-done.7.down_ref = bf16[1216,128]{1,0:T(8,128)(2,1)S(1)} collective-permute-done((bf16[1216,128]{1,0:T(8,128)(2,1)S(1)}, bf16[1216,128]{1,0:T(8,128)(2,1)S(1)}, u32[]{:S(2)}, u32[]{:S(2)}) %collective-permute-start.7) | collective-permute-done | bytes 311328 | tf_op jit(solution)/shard_map/ppermute | solution.py:451
  99.6 1.3 %shard_map.32 = bf16[4,64,1536]{2,1,0:T(8,128)(2,1)} custom-call(f32[256,1792]{1,0:T(8,128)S(1)} %get-tuple-element.16.part_ref, bf16[1216,128]{1,0:T(8,128)(2,1)S(1)} %collective-permute-done.6.up_ref, bf16[1216,128]{1,0:T(8,128)(2,1)S(1)} %collective-permute-done.7.down_ref, f32[16,1792]{1,0:T(8,128)S(1)} %get-tuple-element.22.keep_ref), custom_call_target="tpu_custom_call" | custom-call | flops 4194304 | bytes 4194304 | tf_op jit(solution)/shard_map/pallas_call | solution.py:386
  (7 shorter events, 0.2 us)
Async XLA Ops:
  0.0 1.1 %copy-start = (bf16[4,64,1536]{2,1,0:T(8,128)(2,1)S(1)}, bf16[4,64,1536]{2,1,0:T(8,128)(2,1)}, u32[]{:S(2)}) copy-start(bf16[4,64,1536]{2,1,0:T(8,128)(2,1)} %x_ref.1) | copy-start | bytes 2359300
  1.1 0.7 copy-start.1
  3.9 17.3 %collective-permute-start = (bf16[2896,128]{1,0:T(8,128)(2,1)}, bf16[2896,128]{1,0:T(8,128)(2,1)S(1)}, u32[]{:S(2)}, u32[]{:S(2)}) collective-permute-start(bf16[2896,128]{1,0:T(8,128)(2,1)} %get-tuple-element.26), channel_id=1, source_target_pairs={{0,1},{1,0},{2,3},{3,2},{4,5},{5,4},{6,7},{7,6},{8,9},{9,8},{10,11... | collective-permute-start | bytes 2224136 | tf_op jit(solution)/shard_map/ppermute | solution.py:412
  8.7 29.0 %collective-permute-start.1 = (bf16[2896,128]{1,0:T(8,128)(2,1)S(1)}, bf16[2896,128]{1,0:T(8,128)(2,1)S(1)}, u32[]{:S(2)}, u32[]{:S(2)}) collective-permute-start(bf16[2896,128]{1,0:T(8,128)(2,1)S(1)} %get-tuple-element.25), channel_id=1, source_target_pairs={{0,511},{1,2},{2,1},{3,4},{4,3},{5,6},{6,5},{7,8},{8,7},{9,10},{10... | collective-permute-start | bytes 2224136 | tf_op jit(solution)/shard_map/ppermute | solution.py:411
  37.9 17.3 %collective-permute-start.2 = (bf16[2384,128]{1,0:T(8,128)(2,1)S(1)}, bf16[2384,128]{1,0:T(8,128)(2,1)S(1)}, u32[]{:S(2)}, u32[]{:S(2)}) collective-permute-start(bf16[2384,128]{1,0:T(8,128)(2,1)S(1)} %slice.24), channel_id=1, source_target_pairs={{0,1},{1,2},{2,3},{3,4},{4,5},{5,6},{6,7},{7,8},{8,9},{9,10},{10,1... | collective-permute-start | bytes 1830920 | tf_op jit(solution)/shard_map/ppermute | solution.py:418
  39.9 17.3 %collective-permute-start.4 = (bf16[2384,128]{1,0:T(8,128)(2,1)S(1)}, bf16[2384,128]{1,0:T(8,128)(2,1)S(1)}, u32[]{:S(2)}, u32[]{:S(2)}) collective-permute-start(bf16[2384,128]{1,0:T(8,128)(2,1)S(1)} %slice.26), channel_id=1, source_target_pairs={{0,511},{1,0},{2,1},{3,2},{4,3},{5,4},{6,5},{7,6},{8,7},{9,8},{10,... | collective-permute-start | bytes 1830920 | tf_op jit(solution)/shard_map/ppermute | solution.py:419
  55.3 14.1 %collective-permute-start.3 = (bf16[1872,128]{1,0:T(8,128)(2,1)S(1)}, bf16[1872,128]{1,0:T(8,128)(2,1)S(1)}, u32[]{:S(2)}, u32[]{:S(2)}) collective-permute-start(bf16[1872,128]{1,0:T(8,128)(2,1)S(1)} %slice.25), channel_id=1, source_target_pairs={{0,1},{1,2},{2,3},{3,4},{4,5},{5,6},{6,7},{7,8},{8,9},{9,10},{10,1... | collective-permute-start | bytes 1437704 | tf_op jit(solution)/shard_map/ppermute | solution.py:418
  57.2 12.6 %collective-permute-start.5 = (bf16[1872,128]{1,0:T(8,128)(2,1)S(1)}, bf16[1872,128]{1,0:T(8,128)(2,1)S(1)}, u32[]{:S(2)}, u32[]{:S(2)}) collective-permute-start(bf16[1872,128]{1,0:T(8,128)(2,1)S(1)} %slice.27), channel_id=1, source_target_pairs={{0,511},{1,0},{2,1},{3,2},{4,3},{5,4},{6,5},{7,6},{8,7},{9,8},{10,... | collective-permute-start | bytes 1437704 | tf_op jit(solution)/shard_map/ppermute | solution.py:419
  70.9 27.0 %collective-permute-start.6 = (bf16[1216,128]{1,0:T(8,128)(2,1)S(1)}, bf16[1216,128]{1,0:T(8,128)(2,1)S(1)}, u32[]{:S(2)}, u32[]{:S(2)}) collective-permute-start(bf16[1216,128]{1,0:T(8,128)(2,1)S(1)} %get-tuple-element.20), channel_id=1, source_target_pairs={{0,3},{1,4},{2,5},{3,6},{4,7},{5,8},{6,9},{7,10},{8,11},{9,12},{10... | collective-permute-start | bytes 933896 | tf_op jit(solution)/shard_map/ppermute | solution.py:450
  72.9 26.8 %collective-permute-start.7 = (bf16[1216,128]{1,0:T(8,128)(2,1)S(1)}, bf16[1216,128]{1,0:T(8,128)(2,1)S(1)}, u32[]{:S(2)}, u32[]{:S(2)}) collective-permute-start(bf16[1216,128]{1,0:T(8,128)(2,1)S(1)} %get-tuple-element.21), channel_id=1, source_target_pairs={{0,509},{1,510},{2,511},{3,0},{4,1},{5,2},{6,3},{7,4},{8,5},{9,6},... | collective-permute-start | bytes 933896 | tf_op jit(solution)/shard_map/ppermute | solution.py:451
